TPU v7x, 128 devices: a whole 4x4x4 slice. The times are simulated.
128 devices in a mesh: scan: 16 (over y, z), tile: 8 (over x, core).
Axes of the slice: x: 4, y: 4, z: 4, core: 2. Of those that a mesh axis runs over, the one named last changes fastest.
Arguments:
- object_field: float32 [2, 2048, 4096], P(None, 'tile', 'scan'), may hold values from -4 to 4
- probe_modes: float32 [8, 2, 256, 256], replicated, may hold values from -1.5 to 1.5
- patterns: float32 [512, 256, 256], P(('scan', 'tile')), may hold values from 0.05 to 16
- positions: int32 [512, 2], P(('scan', 'tile')), may hold values from 0 to 4095, as said below
Outputs:
- object_out: float32 [2, 2048, 4096], P(None, 'tile', 'scan')
- probe_out: float32 [8, 2, 256, 256], replicated
Inputs may be any that keep to these rules, and one draw needn't show every extreme that they name: `positions`: pattern j lies on the device of index j // 4 over scan+tile; its row offset lies in [t * 256, (t + 1) * 256) with t that device's tile index. With o = column offset // 256, the owner pairs o and (o + 1) mod the scan axis's size of the patterns of one device are disjoint.
All inputs are finite; a program needn't handle non-finite values.
Results may differ from a plain program's by a relative error of at most 0.00085.
The roundings to bfloat16 on the way count: a program that leaves them out, or rounds other values in their place, can miss the bound.
Values may be sent and summed in bfloat16 or wider, within the bound.
A program may use at most 128 MiB of HBM per device.

v0:
```python
import math

import jax
import jax.numpy as jnp
from jax import lax
from jax.sharding import PartitionSpec as P


def shifted(value, axis, steps):
    count = lax.axis_size(axis)
    pairs = [(source, (source + steps) % count) for source in range(count)]
    return lax.ppermute(value, axis, pairs)


def dft_tables(length):
    counter = jnp.arange(length, dtype=jnp.int32)
    phase = counter[:, None] * counter[None, :] % length
    angle = phase.astype(jnp.float32) * (2.0 * math.pi / length)
    factor = 1.0 / math.sqrt(length)
    return (
        (jnp.cos(angle) * factor).astype(jnp.bfloat16),
        (jnp.sin(angle) * factor).astype(jnp.bfloat16),
    )


def mat_right(real_part, imag_part, cosine, sine_table, sign):

    def product(left_op, right_op):
        return jnp.einsum("mjk,kl->mjl", left_op, right_op, preferred_element_type=jnp.float32)

    real_out = product(real_part, cosine) - sign * product(imag_part, sine_table)
    imag_out = product(imag_part, cosine) + sign * product(real_part, sine_table)
    return (real_out, imag_out)


def mat_left(real_part, imag_part, cosine, sine_table, sign):

    def product(left_op, right_op):
        return jnp.einsum("jk,mkl->mjl", left_op, right_op, preferred_element_type=jnp.float32)

    real_out = product(cosine, real_part) - sign * product(sine_table, imag_part)
    imag_out = product(cosine, imag_part) + sign * product(sine_table, real_part)
    return (real_out, imag_out)


def project(patch_bf, probe_now, pattern, cosine, sine_table):
    probe_re = probe_now[:, 0]
    probe_im = probe_now[:, 1]
    patch_re = patch_bf[0].astype(jnp.float32)
    patch_im = patch_bf[1].astype(jnp.float32)
    wave_re = (probe_re * patch_re - probe_im * patch_im).astype(jnp.bfloat16)
    wave_im = (probe_re * patch_im + probe_im * patch_re).astype(jnp.bfloat16)
    half_re, half_im = mat_right(wave_re, wave_im, cosine, sine_table, -1.0)
    half_re = half_re.astype(jnp.bfloat16)
    half_im = half_im.astype(jnp.bfloat16)
    far_re, far_im = mat_left(half_re, half_im, cosine, sine_table, -1.0)
    power = jnp.sum(far_re * far_re + far_im * far_im, axis=0)
    scaling = jnp.sqrt(pattern) / jnp.sqrt(0.25 + power)
    fixed_re = (far_re * scaling).astype(jnp.bfloat16)
    fixed_im = (far_im * scaling).astype(jnp.bfloat16)
    back_re, back_im = mat_right(fixed_re, fixed_im, cosine, sine_table, 1.0)
    back_re = back_re.astype(jnp.bfloat16)
    back_im = back_im.astype(jnp.bfloat16)
    exit_re, exit_im = mat_left(back_re, back_im, cosine, sine_table, 1.0)
    update_re = jnp.sum(probe_re * exit_re + probe_im * exit_im, axis=0)
    update_im = jnp.sum(probe_re * exit_im - probe_im * exit_re, axis=0)
    update_full = jnp.stack([update_re, update_im], axis=0)
    probe_term = jnp.stack(
        [patch_re * exit_re + patch_im * exit_im, patch_re * exit_im - patch_im * exit_re], axis=1
    )
    patch_power = patch_re * patch_re + patch_im * patch_im
    return (update_full, probe_term, patch_power)


def roll_cols(stacked_block, amount):
    doubled = jnp.concatenate([stacked_block, stacked_block], axis=-1)
    return lax.dynamic_slice_in_dim(doubled, amount, stacked_block.shape[-1], axis=-1)


def body(object_field, probe_modes, patterns, positions):
    scan_count = lax.axis_size("scan")
    scan_index = lax.axis_index("scan")
    tile_index = lax.axis_index("tile")
    patch_side = probe_modes.shape[-1]
    tile_rows = object_field.shape[1]
    per_device = patterns.shape[0]
    cosine, sine_table = dft_tables(patch_side)
    column = jnp.arange(patch_side, dtype=jnp.int32)
    owner_ids = jnp.arange(scan_count, dtype=jnp.int32)
    group_spots = lax.all_gather(positions, "scan", axis=0, tiled=True)
    group_rows = (group_spots[:, 0] - tile_index * tile_rows).reshape(scan_count, per_device)
    group_owner = (group_spots[:, 1] // patch_side).reshape(scan_count, per_device)
    group_shift = (group_spots[:, 1] % patch_side).reshape(scan_count, per_device)
    first_hits = group_owner == scan_index
    second_hits = (group_owner + 1) % scan_count == scan_index
    touch_mask = (first_hits | second_hits).astype(jnp.int32)
    dest_rows = jnp.sum(touch_mask * group_rows, axis=1)
    dest_shift = jnp.sum(touch_mask * group_shift, axis=1)
    dest_first = jnp.any(first_hits, axis=1)
    dest_second = jnp.any(second_hits, axis=1)
    own_rows = positions[:, 0] - tile_index * tile_rows
    own_owner = positions[:, 1] // patch_side
    own_next = (own_owner + 1) % scan_count
    slot_mask = (
        (owner_ids[:, None] == own_owner[None, :]) | (owner_ids[:, None] == own_next[None, :])
    ).astype(jnp.float32)
    object_now = object_field
    probe_now = probe_modes
    rounded = object_now.astype(jnp.bfloat16)
    below_rows = shifted(rounded, "tile", -1)
    extended = jnp.concatenate([rounded, below_rows], axis=1)
    band_rows = lax.all_gather(extended, "scan", axis=2, tiled=True)
    band_rows = jnp.concatenate([band_rows, band_rows[:, :, :patch_side]], axis=2)
    zero_index = jnp.zeros((), jnp.int32)
    patch_list = [
        lax.dynamic_slice(
            band_rows, (zero_index, own_rows[slot], positions[slot, 1]), (2, patch_side, patch_side)
        )
        for slot in range(per_device)
    ]
    probe_numer = jnp.zeros((probe_now.shape[0], 2, patch_side, patch_side), jnp.float32)
    probe_denom = jnp.zeros((patch_side, patch_side), jnp.float32)
    update_list = []
    for slot in range(per_device):
        update_full, probe_term, patch_power = project(
            patch_list[slot], probe_now, patterns[slot], cosine, sine_table
        )
        update_list.append(update_full)
        probe_numer = probe_numer + probe_term
        probe_denom = probe_denom + patch_power
    wave_terms = jnp.stack(update_list, axis=0)
    outgoing = jnp.einsum("ok,kcxy->ocxy", slot_mask, wave_terms, precision=lax.Precision.HIGHEST)
    returned = lax.all_to_all(outgoing, "scan", split_axis=0, concat_axis=0, tiled=True)
    probe_power = jnp.sum(probe_now[:, 0] ** 2 + probe_now[:, 1] ** 2, axis=0)

    def place(slot_index, accum_total):
        wave_term = returned[slot_index]
        stacked_block = jnp.concatenate([wave_term, probe_power[None]], axis=0)
        col_shift = dest_shift[slot_index]
        moved_block = roll_cols(stacked_block, (patch_side - col_shift) % patch_side)
        keep_mask = dest_first[slot_index] & (column >= col_shift) | dest_second[slot_index] & (
            column < col_shift
        )
        moved_block = jnp.where(keep_mask[None, None, :], moved_block, jnp.zeros_like(moved_block))
        row_start = dest_rows[slot_index]
        previous = lax.dynamic_slice_in_dim(accum_total, row_start, patch_side, axis=1)
        return lax.dynamic_update_slice_in_dim(
            accum_total, previous + moved_block, row_start, axis=1
        )

    accum_start = jnp.zeros((3, tile_rows + patch_side, patch_side), jnp.float32)
    accum_total = lax.fori_loop(0, scan_count, place, accum_start)
    spilled = shifted(accum_total[:, tile_rows:, :], "tile", 1)
    own_accum = accum_total[:, :tile_rows, :].at[:, :patch_side, :].add(spilled)
    probe_numer, probe_denom = lax.psum((probe_numer, probe_denom), ("scan", "tile"))
    object_now = (object_now + own_accum[:2]) / (1.0 + own_accum[2])
    probe_now = (probe_now + probe_numer) / (1.0 + probe_denom)
    return (object_now, probe_now)


def solution(mesh):
    return jax.shard_map(
        body,
        mesh=mesh,
        in_specs=(
            P(None, "tile", "scan"),
            P(),
            P(("scan", "tile"), None, None),
            P(("scan", "tile"), None),
        ),
        out_specs=(P(None, "tile", "scan"), P()),
        check_vma=False,
    )
```

profile of v0, /device:TPU:1, one launch (start us, length us, event | category | flops | bytes accessed | tf_op | source)
XLA Modules:
  0.0 676.2 jit_solution(8483409442783738190)
XLA Ops:
  9.8 5.2 collective-permute-done
  29.7 5.4 copy.173
  40.0 56.5 %all-gather.3.cloned.1.call-done = bf16[2,512,4096]{2,1,0:T(8,128)(2,1)} async-done(((bf16[2,512,256]{2,1,0:T(8,128)(2,1)}), bf16[2,512,4096]{2,1,0:T(8,128)(2,1)}) %all-gather.3.cloned.1.call-update) | async-done | bytes 8388624 | tf_op jit(solution)/shard_map/all_gather | solution.py:112
  97.6 2.9 fusion.92
  103.2 2.8 subtract_convert_fusion.11
  126.5 12.2 %convolution_subtract_fusion.3 = f32[8,256,256]{2,1,0:T(8,128)S(1)} fusion(f32[8,256,256]{2,1,0:T(8,128)S(1)} %fusion.192, bf16[8,256,256]{2,1,0:T(8,128)(2,1)S(1)} %add_convert_fusion.9), kind=kOutput, calls=%fused_computation.170 | convolution fusion | flops 270008320 | bytes 5242880 | tf_op jit(solution)/shard_map/jk,mkl->mjl/dot_general | solution.py:39
  140.9 2.0 add_convert_fusion.8
  154.6 1.9 fusion.73
  160.9 2.7 fusion.178
  165.0 2.7 convolution_add_fusion.2
  177.8 1.7 fusion.26
  182.6 1.7 add_convert_fusion
  188.5 2.8 convolution_subtract_fusion
  191.3 2.8 convolution_add_fusion
  196.9 1.8 add_convert_fusion.4
  204.4 1.7 fusion.38
  215.1 2.7 convolution_subtract_fusion.1
  217.8 2.7 convolution_add_fusion.1
  220.5 12.7 %fusion.22 = (f32[8,1,256,256]{2,3,0,1:T(8,128)}, f32[8,1,256,256]{2,3,0,1:T(8,128)}, f32[256,256]{0,1:T(8,128)}, f32[256,256]{0,1:T(8,128)}, f32[256,256]{0,1:T...) fusion(f32[8,256,256]{2,1,0:T(8,128)} %convolution_add_fusion, ...), kind=kOutput, calls=%fused_computation.43 | convolution fusion | flops 297730048 | bytes 38535168 | tf_op jit(solution)/shard_map/jk,mkl->mjl/dot_general | solution.py:39
  236.6 1.8 copy.215
  238.4 1.8 copy.216
  242.4 1.8 copy.195
  246.6 6.0 fusion.9
  252.5 8.3 %copy.259 = f32[16,2,256,256]{3,2,1,0:T(8,128)} copy(f32[16,2,256,256]{3,0,2,1:T(8,128)S(1)} %fusion.9) | data formatting | bytes 16777216 | tf_op jit(solution)/shard_map/ok,kcxy->ocxy/dot_general | solution.py:132
  260.9 4.9 all-to-all-start
  265.8 146.4 %all-gather = s32[16,4,2]{1,2,0:T(2,128)S(1)} all-gather(s32[1,4,2]{1,2,0:T(2,128)S(1)} %bitcast.535), channel_id=1, replica_groups=mesh['scan'=16,'tile'=8] {'scan'}, dimensions={0}, use_global_device_ids=true | all-gather | bytes 544 | tf_op jit(solution)/shard_map/all_gather | solution.py:90
  414.8 2.4 fusion.58
  419.0 4.0 fusion.8
  423.2 221.5 %while.19 = (s32[]{:T(128)}, f32[3,512,256]{2,1,0:T(8,128)S(1)}, s32[16]{0:T(128)S(1)}, pred[16]{0:T(512)(128)(4,1)S(1)}, s32[16]{0:T(128)S(1)}, /*index=5*/pred...) while((s32[]{:T(128)}, f32[3,512,256]{2,1,0:T(8,128)S(1)}, ...), condition=%wide.region_18.19_spmd.clone.clone, body=%wide.region_17.18_spmd.clone.clone.sunk | while | flops 984340 | bytes 4981628 | solution.py:152
  428.2 1.8 and_or_fusion.2
  431.7 5.6 dynamic_update_slice.13
  442.4 1.8 and_or_fusion.2
  445.9 5.6 dynamic_update_slice.13
  456.6 1.8 and_or_fusion.2
  460.1 5.6 dynamic_update_slice.13
  470.7 1.8 and_or_fusion.2
  474.3 5.6 dynamic_update_slice.13
  484.9 1.8 and_or_fusion.2
  488.5 5.7 dynamic_update_slice.13
  499.1 1.8 and_or_fusion.2
  502.7 5.5 dynamic_update_slice.13
  513.1 1.8 and_or_fusion.2
  516.7 5.2 dynamic_update_slice.13
  526.9 1.8 and_or_fusion.2
  530.4 4.1 dynamic_update_slice.13
  539.5 1.8 and_or_fusion.2
  543.1 5.6 dynamic_update_slice.13
  553.7 1.8 and_or_fusion.2
  557.2 5.6 dynamic_update_slice.13
  567.9 1.8 and_or_fusion.2
  571.4 5.6 dynamic_update_slice.13
  582.0 1.8 and_or_fusion.2
  585.6 5.1 dynamic_update_slice.13
  595.7 1.8 and_or_fusion.2
  599.2 5.6 dynamic_update_slice.13
  609.9 1.8 and_or_fusion.2
  613.4 3.6 dynamic_update_slice.13
  622.0 1.8 and_or_fusion.2
  625.6 5.6 dynamic_update_slice.13
  636.2 1.8 and_or_fusion.2
  639.8 4.9 dynamic_update_slice.13
  644.7 9.4 %collective-permute-start.1 = (f32[3,256,256]{2,1,0:T(8,128)S(1)}, f32[3,256,256]{2,1,0:T(8,128)}, u32[]{:S(2)}, u32[]{:S(2)}) collective-permute-start(f32[3,256,256]{2,1,0:T(8,128)S(1)} %slice.153), channel_id=1, source_target_pairs={{0,1},{1,2},{2,3},{3,4},{4,5},{5,6},{6,7},{7,0},{8,9},{9,10},{10,1... | collective-permute-start | bytes 2359304 | tf_op jit(solution)/shard_map/ppermute | solution.py:12
  655.3 6.1 add_divide_fusion
  661.4 5.3 copy.263
  (268 shorter events, 167.2 us)
Async XLA Ops:
  7.2 8.7 %copy-start.28 = (s32[4,2]{0,1:T(2,128)S(1)}, s32[4,2]{0,1:T(2,128)}, u32[]{:S(2)}) copy-start(s32[4,2]{0,1:T(2,128)} %param.13) | copy-start | bytes 100
  7.2 19.7 %copy-start.27 = (f32[4,256,256]{2,1,0:T(8,128)S(1)}, f32[4,256,256]{2,1,0:T(8,128)}, u32[]{:S(2)}) copy-start(f32[4,256,256]{2,1,0:T(8,128)} %param.12) | copy-start | bytes 3145732
  7.2 89.3 %all-gather.3.cloned.1.call-start = ((), (), s32[]{:S(2)}) async-start(), calls=%async_computation.1 | async-start | bytes 8912896 | tf_op jit(solution)/shard_map/all_gather | solution.py:112
  8.4 6.7 collective-permute-start
  100.5 0.7 copy-start.9
  100.5 0.8 copy-start.11
  100.5 1.4 copy-start.13
  100.5 1.4 copy-start.15
  101.7 1.5 copy-start.17
  101.8 4.2 copy-start.18
  138.7 2.2 copy-start
  138.7 2.2 copy-start.7
  140.9 79.6 %copy-start.1 = (f32[8,256,256]{2,1,0:T(8,128)}, f32[8,256,256]{2,1,0:T(8,128)S(1)}, u32[]{:S(2)}) copy-start(f32[8,256,256]{2,1,0:T(8,128)S(1)} %convolution_add_fusion.3) | copy-start | bytes 6291460
  152.8 1.7 copy-start.26
  177.8 1.7 copy-start.25
  204.4 1.7 copy-start.24
  217.8 2.7 copy-start.6
  217.8 2.7 copy-start.8
  233.2 2.6 copy-start.23
  233.2 2.8 copy-start.22
  236.6 7.6 %copy-start.21 = (f32[256,256]{0,1:T(8,128)S(1)}, f32[256,256]{0,1:T(8,128)}, u32[]{:S(2)}) copy-start(f32[256,256]{0,1:T(8,128)} %get-tuple-element.388) | copy-start | bytes 786436
  245.1 1.5 copy-start.20
  260.9 153.0 %copy-start.10 = (bf16[2,256,256]{2,1,0:T(8,128)(2,1)S(1)}, bf16[2,256,256]{2,1,0:T(8,128)(2,1)}, u32[]{:S(2)}) copy-start(bf16[2,256,256]{2,1,0:T(8,128)(2,1)} %copy-done.9) | copy-start | bytes 786436
  260.9 153.0 %copy-start.12 = (bf16[2,256,256]{2,1,0:T(8,128)(2,1)S(1)}, bf16[2,256,256]{2,1,0:T(8,128)(2,1)}, u32[]{:S(2)}) copy-start(bf16[2,256,256]{2,1,0:T(8,128)(2,1)} %copy-done.11) | copy-start | bytes 786436
  260.9 153.0 %copy-start.14 = (bf16[2,256,256]{2,1,0:T(8,128)(2,1)S(1)}, bf16[2,256,256]{2,1,0:T(8,128)(2,1)}, u32[]{:S(2)}) copy-start(bf16[2,256,256]{2,1,0:T(8,128)(2,1)} %copy-done.13) | copy-start | bytes 786436
  260.9 153.0 %copy-start.16 = (bf16[2,256,256]{2,1,0:T(8,128)(2,1)S(1)}, bf16[2,256,256]{2,1,0:T(8,128)(2,1)}, u32[]{:S(2)}) copy-start(bf16[2,256,256]{2,1,0:T(8,128)(2,1)} %copy-done.15) | copy-start | bytes 786436
  260.9 162.2 %all-to-all-start = ((f32[16,2,256,256]{3,2,1,0:T(8,128)}), f32[16,2,256,256]{3,2,1,0:T(8,128)}, u32[]{:S(2)}, u32[]{:S(2)}) async-start(f32[16,2,256,256]{3,2,1,0:T(8,128)} %copy.259), calls=%async_computation | async-start | bytes 16777216 | tf_op jit(solution)/shard_map/all_to_all | solution.py:133
  265.8 388.4 %all-reduce.3.cloned.1.call-start = ((), (), s32[]{:S(2)}) async-start(), calls=%async_computation.2 | async-start | bytes 8912896 | tf_op jit(solution)/shard_map/psum | solution.py:155
  414.8 2.4 copy-start.2
  414.8 3.0 copy-start.3
  414.8 3.6 copy-start.4
  414.8 4.2 copy-start.5
  644.7 22.0 %collective-permute-start.1 = (f32[3,256,256]{2,1,0:T(8,128)S(1)}, f32[3,256,256]{2,1,0:T(8,128)}, u32[]{:S(2)}, u32[]{:S(2)}) collective-permute-start(f32[3,256,256]{2,1,0:T(8,128)S(1)} %slice.153), channel_id=1, source_target_pairs={{0,1},{1,2},{2,3},{3,4},{4,5},{5,6},{6,7},{7,0},{8,9},{9,10},{10,1... | collective-permute-start | bytes 2359304 | tf_op jit(solution)/shard_map/ppermute | solution.py:12
  666.7 1.3 copy-start.19
Sparse Core Ops, SparseCore 0:
  16.0 80.4 all-gather.2
  423.2 163.6 all-reduce.2
where the time goes:
time: 688 us; the launch traced here: 676 us
  local copies, waits for them, and re-layouts  182 us (26%)
  blocking collectives  146 us (21%)
  matrix products  130 us (19%)
  other arithmetic  68.6 us (10%)
  waiting for transfers between devices  61.7 us (9%)
  loops' own time  41.8 us (6%)
  between operations  30 us (4%)
  starting transfers between devices  15.8 us (2%)
    all_gather x1, blocking collectives, body(): group_spots = lax.all_gather(positions, 'scan', axis=0, tiled=True)  146 us
    dynamic_update_slice x16, local copies, waits for them, and re-layouts, place(): lax.dynamic_update_slice_in_dim(accum_total, previous + moved_block, row_...  85 us
    dot_general x32, matrix products, product(): jnp.einsum('jk,mkl->mjl', left_op, right_op, preferred_element_type=jnp.f...  76.1 us
    all_gather x1, waiting for transfers between devices, body(): band_rows = lax.all_gather(extended, 'scan', axis=2, tiled=True)  56.5 us
    dot_general x32, matrix products, product(): jnp.einsum('mjk,kl->mjl', left_op, right_op, preferred_element_type=jnp.f...  47.5 us
    another operation x1, loops' own time, body(): accum_total = lax.fori_loop(0, scan_count, place, accum_start)  41.8 us
    or x16, other arithmetic, place(): dest_first[slot_index] & (column >= col_shift)  29.2 us
    unnamed x66, local copies, waits for them, and re-layouts  18 us
  transfers between devices with their start and end apart: 5, of which 2 were waited for; matrix products, arithmetic and copies ran while one was open for 31% of the time, Pallas kernels for 0%

commit v1 on v0

v1 whole, which is shorter than its diff:
```python
import functools
import math

import jax
import jax.numpy as jnp
import ml_dtypes
import numpy as np
from jax import lax
from jax.experimental import pallas as pl
from jax.experimental.pallas import tpu as pltpu
from jax.sharding import PartitionSpec as P

F32 = jnp.float32
BF16 = jnp.bfloat16
N = 256
H = N // 2


def folded_tables():
    counter = np.arange(N, dtype=np.int32)
    phase = counter[:, None] * counter[None, :] % N
    angle = phase.astype(np.float32) * np.float32(2.0 * math.pi / N)
    factor = np.float32(1.0 / math.sqrt(N))
    cosine = (np.cos(angle) * factor).astype(ml_dtypes.bfloat16)
    sine = (np.sin(angle) * factor).astype(ml_dtypes.bfloat16)
    order = np.where(counter <= H, counter, 3 * H - counter)
    right = np.concatenate([cosine[:, : H + 1], sine[:, 1:H]], axis=1)[order]
    return np.stack([right, np.ascontiguousarray(right.T)])


def dot(left, right):
    return jnp.dot(left, right, preferred_element_type=F32)


def iota(axis):
    return lax.broadcasted_iota(jnp.int32, (N, N), axis)


def folded(index):
    return jnp.where(index <= H, index, 3 * H - index)


def one_hot(condition):
    return jnp.where(condition, 1.0, 0.0).astype(BF16)


def pieces(value, count):
    parts = []
    for _ in range(count):
        part = value.astype(BF16)
        parts.append(part)
        value = value - part.astype(F32)
    return parts


def permute(value, left, right, count):
    rows = sum(dot(left, part) for part in pieces(value, count))
    return sum(dot(part, right) for part in pieces(rows, count))


def fold_cols(a, b, sign):
    first = lax.broadcasted_iota(jnp.int32, (N, H), 1) == 0
    a_lo, a_hi, b_lo, b_hi = a[:, :H], a[:, H:], b[:, :H], b[:, H:]
    a_in = jnp.where(first, 0.0, a_hi)
    b_in = jnp.where(first, 0.0, b_hi)
    re_lo = a_lo - sign * b_in
    im_lo = b_lo + sign * a_in
    re_hi = jnp.where(first, a_hi, a_lo + sign * b_hi)
    im_hi = jnp.where(first, b_hi, b_lo - sign * a_hi)
    return jnp.concatenate([re_lo, re_hi, im_lo, im_hi], axis=1)


def fold_rows(c, sign):
    first = lax.broadcasted_iota(jnp.int32, (H, N), 0) == 0
    a_lo, a_hi, b_lo, b_hi = c[:H, :N], c[H:, :N], c[:H, N:], c[H:, N:]
    a_in = jnp.where(first, 0.0, a_hi)
    b_in = jnp.where(first, 0.0, b_hi)
    re_lo = a_lo - sign * b_in
    im_lo = b_lo + sign * a_in
    re_hi = jnp.where(first, a_hi, a_lo + sign * b_hi)
    im_hi = jnp.where(first, b_hi, b_lo - sign * a_hi)
    return jnp.concatenate([re_lo, re_hi], axis=0), jnp.concatenate([im_lo, im_hi], axis=0)


def transform(re, im, table, sign):
    right = table[0]
    half = fold_cols(dot(re, right), dot(im, right), sign).astype(BF16)
    return fold_rows(dot(table[1], half), sign)


def project_kernel(
    pos, near, far_block, below, pattern, probe, table, slots, numer, denom, folded_probe, far, power, patch, update
):
    step = pl.program_id(0)
    modes = probe.shape[0]
    row_shift, col_shift = pos[step, 0] % N, pos[step, 1] % N
    pair = pos[step, 1] // (2 * N)
    rows, cols = iota(0), iota(1)
    fold_matrix = one_hot(rows == folded(cols))

    @pl.when(step == 0)
    def _():
        slots[...] = jnp.zeros_like(slots)
        numer[...] = jnp.zeros_like(numer)
        denom[...] = jnp.zeros_like(denom)

        @pl.loop(0, modes)
        def _(m):
            for plane in range(2):
                folded_probe[m, plane] = permute(probe[m, plane], fold_matrix, fold_matrix, 3)

    row_pick = one_hot(cols == (row_shift + folded(rows)) % N)
    row_back = one_hot(rows == (row_shift + folded(cols)) % N)
    col_pick = one_hot(rows == (col_shift + folded(cols)) % N)
    col_back = one_hot(cols == (col_shift + folded(rows)) % N)
    for plane in range(2):
        top = jnp.where(cols >= col_shift, near[0, plane].astype(F32), far_block[0, plane].astype(F32))
        window = jnp.where(rows >= row_shift, top, below[0, plane].astype(F32)).astype(BF16)
        patch[plane] = dot(dot(row_pick, window).astype(BF16), col_pick)
    power[...] = jnp.full_like(power, 0.25)

    @pl.loop(0, modes)
    def _(m):
        p_re, p_im = folded_probe[m, 0], folded_probe[m, 1]
        o_re, o_im = patch[0], patch[1]
        wave_re = (p_re * o_re - p_im * o_im).astype(BF16)
        wave_im = (p_re * o_im + p_im * o_re).astype(BF16)
        f_re, f_im = transform(wave_re, wave_im, table, -1.0)
        far[m, 0] = f_re
        far[m, 1] = f_im
        power[...] += f_re * f_re + f_im * f_im

    level = permute(pattern[0], fold_matrix, fold_matrix, 3)
    power[...] = jnp.sqrt(level) / jnp.sqrt(power[...])
    update[...] = jnp.zeros_like(update)

    @pl.loop(0, modes)
    def _(m):
        scaling = power[...]
        fixed_re = (far[m, 0] * scaling).astype(BF16)
        fixed_im = (far[m, 1] * scaling).astype(BF16)
        e_re, e_im = transform(fixed_re, fixed_im, table, 1.0)
        p_re, p_im = folded_probe[m, 0], folded_probe[m, 1]
        update[0] += p_re * e_re + p_im * e_im
        update[1] += p_re * e_im - p_im * e_re
        o_re, o_im = patch[0], patch[1]
        numer[m, 0] += o_re * e_re + o_im * e_im
        numer[m, 1] += o_re * e_im - o_im * e_re

    denom[...] += patch[0] * patch[0] + patch[1] * patch[1]
    for plane in range(2):
        slots[2 * pair + plane] = permute(update[plane], row_back, col_back, 2)

    @pl.when(step == pl.num_programs(0) - 1)
    def _():
        @pl.loop(0, modes)
        def _(m):
            for plane in range(2):
                numer[m, plane] = permute(numer[m, plane], fold_matrix, fold_matrix, 2)

        denom[...] = permute(denom[...], fold_matrix, fold_matrix, 2)


def project(positions, band, below, patterns, probe, table):
    count, (modes,) = patterns.shape[0], probe.shape[:1]
    blocks = band.shape[0]
    whole = lambda shape: pl.BlockSpec(shape, lambda k, pos: (0,) * len(shape))
    near = pl.BlockSpec((1, 2, N, N), lambda k, pos: (pos[k, 1] // N, 0, 0, 0))
    after = pl.BlockSpec((1, 2, N, N), lambda k, pos: ((pos[k, 1] // N + 1) % blocks, 0, 0, 0))
    return pl.pallas_call(
        project_kernel,
        grid_spec=pltpu.PrefetchScalarGridSpec(
            num_scalar_prefetch=1,
            grid=(count,),
            in_specs=[
                near,
                after,
                pl.BlockSpec((1, 2, N, N), lambda k, pos: (k, 0, 0, 0)),
                pl.BlockSpec((1, N, N), lambda k, pos: (k, 0, 0)),
                whole((modes, 2, N, N)),
                whole((2, N, N)),
            ],
            out_specs=[whole((blocks, N, N)), whole((modes, 2, N, N)), whole((N, N))],
            scratch_shapes=[
                pltpu.VMEM((modes, 2, N, N), F32),
                pltpu.VMEM((modes, 2, N, N), F32),
                pltpu.VMEM((N, N), F32),
                pltpu.VMEM((2, N, N), F32),
                pltpu.VMEM((2, N, N), F32),
            ],
        ),
        out_shape=[
            jax.ShapeDtypeStruct((blocks, N, N), F32),
            jax.ShapeDtypeStruct((modes, 2, N, N), F32),
            jax.ShapeDtypeStruct((N, N), F32),
        ],
        compiler_params=pltpu.CompilerParams(vmem_limit_bytes=60 * 2**20),
        name="project",
    )(positions, band, band, below, patterns, probe, table)


def cut_kernel(pos, near, after, out):
    step = pl.program_id(0)
    col_shift = pos[step, 1] % N
    cols = iota(1)
    for plane in range(2):
        out[0, plane] = jnp.where(
            cols >= col_shift, near[0, plane].astype(F32), after[0, plane].astype(F32)
        ).astype(BF16)


def cut(positions, band):
    count, blocks = positions.shape[0], band.shape[0]
    return pl.pallas_call(
        cut_kernel,
        grid_spec=pltpu.PrefetchScalarGridSpec(
            num_scalar_prefetch=1,
            grid=(count,),
            in_specs=[
                pl.BlockSpec((1, 2, N, N), lambda k, pos: (pos[k, 1] // N, 0, 0, 0)),
                pl.BlockSpec((1, 2, N, N), lambda k, pos: ((pos[k, 1] // N + 1) % blocks, 0, 0, 0)),
            ],
            out_specs=pl.BlockSpec((1, 2, N, N), lambda k, pos: (k, 0, 0, 0)),
        ),
        out_shape=jax.ShapeDtypeStruct((count, 2, N, N), BF16),
        name="cut",
    )(positions, band, band)


def cover_kernel(place, pos_own, pos_above, probe, out):
    me, blocks = place[0], place[1]
    rows, cols = iota(0), iota(1)
    total = jnp.zeros((N, N), F32)
    for m in range(probe.shape[0]):
        total = total + (probe[m, 0] * probe[m, 0] + probe[m, 1] * probe[m, 1])
    out[...] = jnp.zeros_like(out)

    for above, pos in ((False, pos_own), (True, pos_above)):
        @pl.loop(0, pos_own.shape[0])
        def _(k):
            owner = pos[k, 1] // N
            row_shift, col_shift = pos[k, 0] % N, pos[k, 1] % N
            head, tail = owner == me, (owner + 1) % blocks == me

            @pl.when(head | tail)
            def _():
                moved = pltpu.roll(pltpu.roll(total, row_shift, 0), col_shift, 1)
                keep = (rows < row_shift) if above else (rows >= row_shift)
                split = jnp.where(head, col_shift, 0)
                stop = jnp.where(head, N, col_shift)
                keep = keep & (cols >= split) & (cols < stop)
                out[...] += jnp.where(keep, moved, 0.0)


def cover_of(place, pos_own, pos_above, probe):
    whole = lambda shape: pl.BlockSpec(shape, lambda i, *_: (0,) * len(shape))
    return pl.pallas_call(
        cover_kernel,
        grid_spec=pltpu.PrefetchScalarGridSpec(
            num_scalar_prefetch=3, grid=(1,), in_specs=[whole(probe.shape)], out_specs=whole((N, N))
        ),
        out_shape=jax.ShapeDtypeStruct((N, N), F32),
        compiler_params=pltpu.CompilerParams(vmem_limit_bytes=40 * 2**20),
        name="cover",
    )(place, pos_own, pos_above, probe)


def gather_kernel_sum(place, pos, received, out):
    pair = place[0] // 2
    rows, cols = iota(0), iota(1)
    out[...] = jnp.zeros_like(out)
    per_device = pos.shape[0] // received.shape[0]

    @pl.loop(0, pos.shape[0])
    def _(k):
        owner = pos[k, 1] // N
        row_shift, col_shift = pos[k, 0] % N, pos[k, 1] % N
        side = owner - 2 * pair

        @pl.when((side == 0) | (side == 1))
        def _():
            value = received[k // per_device]
            low, right = rows < row_shift, cols >= col_shift
            out[0, side] += jnp.where(low, 0.0, jnp.where(right, value, 0.0))
            out[0, side + 1] += jnp.where(low, 0.0, jnp.where(right, 0.0, value))
            out[1, side] += jnp.where(low, jnp.where(right, value, 0.0), 0.0)
            out[1, side + 1] += jnp.where(low, jnp.where(right, 0.0, value), 0.0)


def collect(place, pos, received):
    whole = lambda shape: pl.BlockSpec(shape, lambda i, *_: (0,) * len(shape))
    return pl.pallas_call(
        gather_kernel_sum,
        grid_spec=pltpu.PrefetchScalarGridSpec(
            num_scalar_prefetch=2, grid=(1,), in_specs=[whole(received.shape)], out_specs=whole((2, 3, N, N))
        ),
        out_shape=jax.ShapeDtypeStruct((2, 3, N, N), F32),
        compiler_params=pltpu.CompilerParams(vmem_limit_bytes=40 * 2**20),
        name="collect",
    )(place, pos, received)


def shifted(value, axis, steps):
    count = lax.axis_size(axis)
    return lax.ppermute(value, axis, [(s, (s + steps) % count) for s in range(count)])


def body(object_field, probe_modes, patterns, positions):
    scan_count, tile_count = lax.axis_size("scan"), lax.axis_size("tile")
    me, tile = lax.axis_index("scan"), lax.axis_index("tile")
    table = jnp.asarray(folded_tables())
    place = jnp.stack([me, jnp.int32(scan_count)])
    pos_all = lax.all_gather(positions, ("scan", "tile"), axis=0, tiled=True)
    pos_all = pos_all.reshape(scan_count, tile_count, -1, 2)
    above_tile = (tile + tile_count - 1) % tile_count
    pos_own = lax.dynamic_index_in_dim(pos_all, tile, 1, keepdims=False)
    pos_above = lax.dynamic_index_in_dim(pos_all, above_tile, 1, keepdims=False)
    pos_prev = lax.dynamic_index_in_dim(pos_above, me, 0, keepdims=False)
    pos_own = pos_own.reshape(-1, 2)
    pos_above = pos_above.reshape(-1, 2)
    band = lax.all_gather(object_field.astype(BF16), "scan", axis=0, tiled=False)
    below = shifted(cut(pos_prev, band), "tile", -1)
    slots, numer, denom = project(positions, band, below, patterns, probe_modes, table)
    received = lax.all_to_all(slots, "scan", split_axis=0, concat_axis=0, tiled=True)
    cover = cover_of(place, pos_own, pos_above, probe_modes)
    numer, denom = lax.psum((numer, denom), ("scan", "tile"))
    sums = collect(place, pos_own, received)
    sums = sums[0] + shifted(sums[1], "tile", 1)
    odd = me % 2 == 1
    swapped = lax.ppermute(jnp.where(odd, sums[0], sums[1]), "scan", [(s, s ^ 1) for s in range(scan_count)])
    tail_re = lax.ppermute(sums[2], "scan", [(s, (s + 2) % scan_count) for s in range(0, scan_count, 2)])
    tail_im = lax.ppermute(sums[2], "scan", [(s, (s + 1) % scan_count) for s in range(1, scan_count, 2)])
    whole_re = jnp.where(odd, swapped, sums[0] + tail_re)
    whole_im = jnp.where(odd, sums[1], swapped + tail_im)
    object_now = (object_field + jnp.stack([whole_re, whole_im])) / (1.0 + cover)
    probe_now = (probe_modes + numer) / (1.0 + denom)
    return (object_now, probe_now)


def solution(mesh):
    return jax.shard_map(
        body,
        mesh=mesh,
        in_specs=(
            P(None, "tile", "scan"),
            P(),
            P(("scan", "tile"), None, None),
            P(("scan", "tile"), None),
        ),
        out_specs=(P(None, "tile", "scan"), P()),
        check_vma=False,
    )
```

time: 688 us -> 378 us (0.55); the launches traced: 676 us -> 377 us
  local copies, waits for them, and re-layouts: 182 us -> 5.27 us
  waiting for transfers between devices: 61.7 us -> 213 us
  matrix products: 130 us -> 0 us
  blocking collectives: 146 us -> 38.7 us
  Pallas kernels: 0 us -> 79.8 us
  other arithmetic: 68.6 us -> 8.95 us
  loops' own time: 41.8 us -> 0 us
  between operations: 30 us -> 14.2 us
    dot_general x65 -> x0, matrix products: 130 us -> none  [the longest x32 76.1 us: product(): jnp.einsum('jk,mkl->mjl', left_op, right_op, preferred_element_type=jnp.f...]
    psum x1, waiting for transfers between devices: 0.01 us -> 118 us  [body(): numer, denom = lax.psum((numer, denom), ('scan', 'tile'))]
    all_gather x1, blocking collectives: 146 us -> 38.7 us  [body(): pos_all = lax.all_gather(positions, ('scan', 'tile'), axis=0, tiled=True)]
    dynamic_update_slice x16 -> x0, local copies, waits for them, and re-layouts: 85 us -> none  [place(): lax.dynamic_update_slice_in_dim(accum_total, previous + moved_block, row_...]
    pallas_call x0 -> x4, Pallas kernels: none -> 79.8 us  [the longest x1 60.9 us: project(): pl.pallas_call(project_kernel, grid_spec=pltpu.PrefetchScalarGridSpec(num...]
    all_to_all x1, waiting for transfers between devices: 0.01 us -> 56.4 us  [body(): lax.all_to_all(slots, 'scan', split_axis=0, concat_axis=0, tiled=True)]
    another operation x1 -> x0, loops' own time: 41.8 us -> none  [body(): accum_total = lax.fori_loop(0, scan_count, place, accum_start)]
    all_gather x1, waiting for transfers between devices: 56.5 us -> 17.3 us  [body(): lax.all_gather(object_field.astype(BF16), 'scan', axis=0, tiled=False)]
  transfers between devices with their start and end apart: 5 -> 8, of which waited for: 2 -> 6; matrix products, arithmetic and copies ran while one was open for 31% -> 2% of each run, Pallas kernels for 0% -> 4%
where the time goes in v1:
time: 378 us; the launch traced here: 377 us
  waiting for transfers between devices  213 us (56%)
  Pallas kernels  79.8 us (21%)
  blocking collectives  38.7 us (10%)
  starting transfers between devices  17.3 us (5%)
  between operations  14.2 us (4%)
  other arithmetic  8.95 us (2%)
  local copies, waits for them, and re-layouts  5.27 us (1%)
    psum x1, waiting for transfers between devices, body(): numer, denom = lax.psum((numer, denom), ('scan', 'tile'))  118 us
    pallas_call x1, Pallas kernels, project(): pl.pallas_call(project_kernel, grid_spec=pltpu.PrefetchScalarGridSpec(num...  60.9 us
    all_to_all x1, waiting for transfers between devices, body(): lax.all_to_all(slots, 'scan', split_axis=0, concat_axis=0, tiled=True)  56.4 us
    all_gather x1, blocking collectives, body(): pos_all = lax.all_gather(positions, ('scan', 'tile'), axis=0, tiled=True)  38.7 us
    all_gather x1, waiting for transfers between devices, body(): lax.all_gather(object_field.astype(BF16), 'scan', axis=0, tiled=False)  17.3 us
    ppermute x2, waiting for transfers between devices, shifted(): lax.ppermute(value, axis, [(s, (s + steps) % count) for s in range(count)])  13.1 us
    pallas_call x1, Pallas kernels, cover_of(): pl.pallas_call(cover_kernel, grid_spec=pltpu.PrefetchScalarGridSpec(num_s...  8.66 us
  transfers between devices with their start and end apart: 8, of which 6 were waited for; matrix products, arithmetic and copies ran while one was open for 2% of the time, Pallas kernels for 4%

profile of v1, /device:TPU:1, one launch (start us, length us, event | category | flops | bytes accessed | tf_op | source)
XLA Modules:
  0.0 376.9 jit_solution(3970872354269330509)
XLA Ops:
  7.2 0.0 all-gather.4.cloned.1.call-start
  7.2 1.8 convert_element_type.3
  9.0 0.0 all-gather.4.cloned.1.call-update
  9.0 38.7 %all-gather.1 = s32[128,4,2]{1,2,0:T(2,128)S(1)} all-gather(s32[1,4,2]{1,2,0:T(2,128)} %bitcast.41), channel_id=1, replica_groups=mesh['scan'=16,'tile'=8] {'scan','tile'}, dimensions={0}, use_global_device_ids=true | all-gather | bytes 4128 | tf_op jit(solution)/shard_map/all_gather | solution.py:313
  47.7 0.7 copy.22.pos
  48.4 17.3 %all-gather.4.cloned.1.call-done = bf16[32,256,256]{2,1,0:T(8,128)(2,1)} async-done(((bf16[2,256,256]{2,1,0:T(8,128)(2,1)}), bf16[32,256,256]{2,1,0:T(8,128)(2,1)}) %all-gather.4.cloned.1.call-update) | async-done | bytes 4194320 | tf_op jit(solution)/shard_map/all_gather | solution.py:321
  65.7 0.0 copy-start.4
  65.7 4.5 %cut.1 = bf16[4,2,256,256]{3,2,1,0:T(8,128)(2,1)} custom-call(s32[4,2]{1,0:T(4,128)} %copy.22.pos, bf16[16,2,256,256]{3,2,1,0:T(8,128)(2,1)} %bitcast.35, bf16[16,2,256,256]{3,2,1,0:T(8,128)(2,1)} %bitcast.36), custom_call_target="tpu_custom_call" | custom-call | tf_op jit(solution)/shard_map/cut/pallas_call | solution.py:214
  70.2 0.7 collective-permute-start
  70.9 0.0 copy-done.4
  70.9 0.7 copy.23.pos
  71.5 13.1 %collective-permute-done.below = bf16[4,2,256,256]{3,2,1,0:T(8,128)(2,1)S(1)} collective-permute-done((bf16[4,2,256,256]{3,2,1,0:T(8,128)(2,1)}, bf16[4,2,256,256]{3,2,1,0:T(8,128)(2,1)S(1)}, u32[]{:S(2)}, u32[]{:S(2)}) %collective-permute-start) | collective-permute-done | bytes 1048608 | tf_op jit(solution)/shard_map/ppermute | solution.py:305
  84.6 0.0 copy-start.3
  84.6 1.1 copy-done.3
  85.7 60.9 %project.1 = (f32[16,256,256]{2,1,0:T(8,128)}, f32[8,2,256,256]{3,2,1,0:T(8,128)}, f32[256,256]{1,0:T(8,128)}) custom-call(s32[4,2]{1,0:T(4,128)} %copy.23.pos, bf16[16,2,256,256]{3,2,1,0:T(8,128)(2,1)} %bitcast.37, bf16[16,2,256,256]{3,2,1,0:T(8,128)(2,1)} %bitcast.38, bf16[4,2,256,256]{3,2,1,0:T(8,128)(2,1)} %copy-done.3, f32[4,256,256]{2,1,0:T(8,128)} %pattern.1, ...), custom_call_target="tpu_custom_call" | custom-call | tf_op jit(solution)/shard_map/project/pallas_call | solution.py:170
  146.6 5.1 %all-to-all-start = ((f32[16,256,256]{2,1,0:T(8,128)}), f32[16,256,256]{2,1,0:T(8,128)}, u32[]{:S(2)}, u32[]{:S(2)}) async-start(f32[16,256,256]{2,1,0:T(8,128)} %get-tuple-element.5), calls=%async_computation | async-start | bytes 8388608 | tf_op jit(solution)/shard_map/all_to_all | solution.py:324
  151.7 0.0 all-reduce.3.cloned.1.call-start
  151.7 0.7 all-reduce.3.cloned.1.call-update
  152.5 0.2 copy.28
  152.7 0.1 pad_add_fusion.place
  152.7 56.4 %all-to-all-done.received = f32[16,256,256]{2,1,0:T(8,128)} async-done(((f32[16,256,256]{2,1,0:T(8,128)}), f32[16,256,256]{2,1,0:T(8,128)}, u32[]{:S(2)}, u32[]{:S(2)}) %all-to-all-start) | async-done | bytes 4194336 | tf_op jit(solution)/shard_map/all_to_all | solution.py:324
  209.1 5.7 %collect.1 = f32[2,3,256,256]{3,2,1,0:T(8,128)S(1)} custom-call(s32[2]{0:T(128)S(1)} %pad_add_fusion.place, s32[64,2]{1,0:T(8,128)S(1)} %bitcast.32, f32[16,256,256]{2,1,0:T(8,128)} %all-to-all-done.received), custom_call_target="tpu_custom_call" | custom-call | tf_op jit(solution)/shard_map/collect/pallas_call | solution.py:292
  214.8 0.1 slice_bitcast_fusion
  214.9 4.9 %collective-permute-start.1 = (f32[3,256,256]{2,1,0:T(8,128)S(1)}, f32[3,256,256]{2,1,0:T(8,128)S(1)}, u32[]{:S(2)}, u32[]{:S(2)}) collective-permute-start(f32[3,256,256]{2,1,0:T(8,128)S(1)} %slice_bitcast_fusion), channel_id=1, source_target_pairs={{0,1},{1,2},{2,3},{3,4},{4,5},{5,6},{6,7},{7,0},{8,9},{9,10},{10,1... | collective-permute-start | bytes 2359304 | tf_op jit(solution)/shard_map/ppermute | solution.py:305
  219.8 0.2 copy.30
  220.0 0.0 copy-start
  220.0 2.3 copy-done
  222.3 8.7 %cover.1 = f32[256,256]{1,0:T(8,128)S(1)} custom-call(s32[2]{0:T(128)S(1)} %pad_add_fusion.place, s32[64,2]{1,0:T(8,128)S(1)} %bitcast.33, s32[64,2]{1,0:T(8,128)S(1)} %bitcast.34, f32[8,2,256,256]{3,2,1,0:T(8,128)S(1)} %copy-done), custom_call_target="tpu_custom_call" | custom-call | tf_op jit(solution)/shard_map/cover/pallas_call | solution.py:257
  231.0 118.5 %all-reduce.3.cloned.1.call-done = (f32[8,2,256,256]{3,2,1,0:T(8,128)}, f32[256,256]{1,0:T(8,128)}) async-done(((f32[8,2,256,256]{3,2,1,0:T(8,128)}, f32[256,256]{1,0:T(8,128)}), (f32[8,2,256,256]{3,2,1,0:T(8,128)}, f32[256,256]{1,0:T(8,128)})) %all-reduce.3.cloned.1.call-update) | async-done | bytes 4456464 | tf_op jit(solution)/shard_map/psum | solution.py:326
  349.4 0.0 copy-start.1
  349.4 1.1 broadcast_add_fusion
  350.6 0.0 collective-permute-done.1
  350.6 0.1 fusion
  350.7 4.3 %collective-permute-start.3 = (f32[256,256]{1,0:T(8,128)S(1)}, f32[256,256]{1,0:T(8,128)S(1)}, u32[]{:S(2)}, u32[]{:S(2)}) collective-permute-start(f32[256,256]{1,0:T(8,128)S(1)} %slice_bitcast_fusion.2), channel_id=1, source_target_pairs={{0,16},{16,32},{32,48},{48,64},{64,80},{80,96},{96,112},{112,0},{1... | collective-permute-start | bytes 786440 | tf_op jit(solution)/shard_map/ppermute | solution.py:331
  355.0 1.3 collective-permute-start.4
  356.4 1.0 collective-permute-start.2
  357.3 0.0 copy-done.1
  357.4 0.0 copy-start.2
  357.4 4.9 %add_divide_fusion = f32[8,2,256,256]{3,2,1,0:T(8,128)} fusion(f32[8,2,256,256]{3,2,1,0:T(8,128)S(1)} %copy-done.1, f32[8,2,256,256]{3,2,1,0:T(8,128)} %get-tuple-element.8, f32[256,256]{1,0:T(8,128)S(1)} %broadcast_add_fusion), kind=kLoop, calls=%fused_computation | loop fusion | flops 2097152 | bytes 12845056 | tf_op jit(solution)/shard_map/div | solution.py:336
  362.2 3.7 collective-permute-done.2
  365.9 0.0 collective-permute-done.3
  365.9 3.2 collective-permute-done.4
  369.1 0.1 select_bitcast_fusion.1
  369.2 0.0 copy-done.2
  369.2 0.9 fusion.1
  (5 shorter events, 0.1 us)
Async XLA Ops:
  7.2 58.5 %all-gather.4.cloned.1.call-start = ((), (), s32[]{:S(2)}) async-start(), calls=%async_computation.1 | async-start | bytes 4456448 | tf_op jit(solution)/shard_map/all_gather | solution.py:321
  65.7 5.2 %copy-start.4 = (s32[4,2]{0,1:T(2,128)S(1)}, s32[4,2]{0,1:T(2,128)}, u32[]{:S(2)}) copy-start(s32[4,2]{0,1:T(2,128)} %param.8) | copy-start | bytes 100
  70.2 14.4 %collective-permute-start = (bf16[4,2,256,256]{3,2,1,0:T(8,128)(2,1)}, bf16[4,2,256,256]{3,2,1,0:T(8,128)(2,1)S(1)}, u32[]{:S(2)}, u32[]{:S(2)}) collective-permute-start(bf16[4,2,256,256]{3,2,1,0:T(8,128)(2,1)} %cut.1), channel_id=1, source_target_pairs={{0,7},{1,0},{2,1},{3,2},{4,3},{5,4},{6,5},{7,6},{8,15},{9,8},{10,9... | collective-permute-start | bytes 3145736 | tf_op jit(solution)/shard_map/ppermute | solution.py:305
  84.6 1.1 copy-start.3
  146.6 62.5 %all-to-all-start = ((f32[16,256,256]{2,1,0:T(8,128)}), f32[16,256,256]{2,1,0:T(8,128)}, u32[]{:S(2)}, u32[]{:S(2)}) async-start(f32[16,256,256]{2,1,0:T(8,128)} %get-tuple-element.5), calls=%async_computation | async-start | bytes 8388608 | tf_op jit(solution)/shard_map/all_to_all | solution.py:324
  151.7 197.8 %all-reduce.3.cloned.1.call-start = ((), (), s32[]{:S(2)}) async-start(), calls=%async_computation.2 | async-start | bytes 8912896 | tf_op jit(solution)/shard_map/psum | solution.py:326
  214.9 135.7 %collective-permute-start.1 = (f32[3,256,256]{2,1,0:T(8,128)S(1)}, f32[3,256,256]{2,1,0:T(8,128)S(1)}, u32[]{:S(2)}, u32[]{:S(2)}) collective-permute-start(f32[3,256,256]{2,1,0:T(8,128)S(1)} %slice_bitcast_fusion), channel_id=1, source_target_pairs={{0,1},{1,2},{2,3},{3,4},{4,5},{5,6},{6,7},{7,0},{8,9},{9,10},{10,1... | collective-permute-start | bytes 2359304 | tf_op jit(solution)/shard_map/ppermute | solution.py:305
  220.0 2.3 copy-start
  349.4 7.9 %copy-start.1 = (f32[8,2,256,256]{3,2,1,0:T(8,128)S(1)}, f32[8,2,256,256]{3,2,1,0:T(8,128)}, u32[]{:S(2)}) copy-start(f32[8,2,256,256]{3,2,1,0:T(8,128)} %probe.3) | copy-start | bytes 12582916
  350.7 15.2 %collective-permute-start.3 = (f32[256,256]{1,0:T(8,128)S(1)}, f32[256,256]{1,0:T(8,128)S(1)}, u32[]{:S(2)}, u32[]{:S(2)}) collective-permute-start(f32[256,256]{1,0:T(8,128)S(1)} %slice_bitcast_fusion.2), channel_id=1, source_target_pairs={{0,16},{16,32},{32,48},{48,64},{64,80},{80,96},{96,112},{112,0},{1... | collective-permute-start | bytes 786440 | tf_op jit(solution)/shard_map/ppermute | solution.py:331
  355.0 14.1 %collective-permute-start.4 = (f32[256,256]{1,0:T(8,128)S(1)}, f32[256,256]{1,0:T(8,128)S(1)}, u32[]{:S(2)}, u32[]{:S(2)}) collective-permute-start(f32[256,256]{1,0:T(8,128)S(1)} %slice_bitcast_fusion.2), channel_id=1, source_target_pairs={{8,16},{24,32},{40,48},{56,64},{72,80},{88,96},{104,112},{120,0},{... | collective-permute-start | bytes 786440 | tf_op jit(solution)/shard_map/ppermute | solution.py:332
  356.4 9.5 %collective-permute-start.2 = (f32[256,256]{1,0:T(8,128)S(1)}, f32[256,256]{1,0:T(8,128)S(1)}, u32[]{:S(2)}, u32[]{:S(2)}) collective-permute-start(f32[256,256]{1,0:T(8,128)S(1)} %fusion.2), channel_id=1, source_target_pairs={{0,8},{8,0},{16,24},{24,16},{32,40},{40,32},{48,56},{56,48},{64,72... | collective-permute-start | bytes 786440 | tf_op jit(solution)/shard_map/ppermute | solution.py:330
  357.4 11.8 %copy-start.2 = (f32[2,256,256]{2,1,0:T(8,128)S(1)}, f32[2,256,256]{2,1,0:T(8,128)}, u32[]{:S(2)}) copy-start(f32[2,256,256]{2,1,0:T(8,128)} %param.5) | copy-start | bytes 1572868
Sparse Core Ops, SparseCore 0:
  10.7 54.9 all-gather.3
  158.2 191.2 all-reduce.2

commit v2 on v1

--- a/solution.py
+++ b/solution.py
@@ -14,6 +14,10 @@
 BF16 = jnp.bfloat16
 N = 256
 H = N // 2
+I16 = jnp.int16
+TAIL = 16
+FULL = 32767.0
+MESH = pl.DeviceIdType.MESH
 
 
 def folded_tables():
@@ -58,6 +62,27 @@
     return sum(dot(part, right) for part in pieces(rows, count))
 
 
+def encode(value):
+    size = jnp.abs(value)
+    peak = jnp.maximum(jnp.max(size, axis=0, keepdims=True), 1e-30)
+    exponent = jnp.ceil(jnp.log(peak) * (1.0 / math.log(2.0)) + 1e-5)
+    scale = jnp.exp(exponent * -math.log(2.0))
+    code = jnp.minimum(jnp.sqrt(size * scale) * FULL + 0.5, FULL).astype(jnp.int32)
+    code = jnp.where(value < 0.0, -code, code).astype(I16)
+    tail = jnp.broadcast_to(exponent.astype(jnp.int32), (TAIL, value.shape[1])).astype(I16)
+    return code, tail
+
+
+def decode_scale(tail):
+    exponent = tail.astype(jnp.int32).astype(F32)[:1]
+    return jnp.exp(exponent * math.log(2.0)) * (1.0 / (FULL * FULL))
+
+
+def decode(code, scale):
+    code = code.astype(jnp.int32).astype(F32)
+    return code * jnp.abs(code) * scale
+
+
 def fold_cols(a, b, sign):
     first = lax.broadcasted_iota(jnp.int32, (N, H), 1) == 0
     a_lo, a_hi, b_lo, b_hi = a[:, :H], a[:, H:], b[:, :H], b[:, H:]
@@ -89,7 +114,7 @@
 
 
 def project_kernel(
-    pos, near, far_block, below, pattern, probe, table, slots, numer, denom, folded_probe, far, power, patch, update
+    pos, near, far_block, below, pattern, probe, table, slots, sums, folded_probe, far, power, patch, update
 ):
     step = pl.program_id(0)
     modes = probe.shape[0]
@@ -101,8 +126,7 @@
     @pl.when(step == 0)
     def _():
         slots[...] = jnp.zeros_like(slots)
-        numer[...] = jnp.zeros_like(numer)
-        denom[...] = jnp.zeros_like(denom)
+        sums[...] = jnp.zeros_like(sums)
 
         @pl.loop(0, modes)
         def _(m):
@@ -144,21 +168,20 @@
         update[0] += p_re * e_re + p_im * e_im
         update[1] += p_re * e_im - p_im * e_re
         o_re, o_im = patch[0], patch[1]
-        numer[m, 0] += o_re * e_re + o_im * e_im
-        numer[m, 1] += o_re * e_im - o_im * e_re
-
-    denom[...] += patch[0] * patch[0] + patch[1] * patch[1]
+        sums[2 * m] += o_re * e_re + o_im * e_im
+        sums[2 * m + 1] += o_re * e_im - o_im * e_re
+
+    sums[2 * modes] += patch[0] * patch[0] + patch[1] * patch[1]
     for plane in range(2):
-        slots[2 * pair + plane] = permute(update[plane], row_back, col_back, 2)
+        code, exponent = encode(permute(update[plane], row_back, col_back, 2))
+        slots[2 * pair + plane, :N] = code
+        slots[2 * pair + plane, N:] = exponent
 
     @pl.when(step == pl.num_programs(0) - 1)
     def _():
-        @pl.loop(0, modes)
+        @pl.loop(0, 2 * modes + 1)
         def _(m):
-            for plane in range(2):
-                numer[m, plane] = permute(numer[m, plane], fold_matrix, fold_matrix, 2)
-
-        denom[...] = permute(denom[...], fold_matrix, fold_matrix, 2)
+            sums[m] = permute(sums[m], fold_matrix, fold_matrix, 2)
 
 
 def project(positions, band, below, patterns, probe, table):
@@ -180,7 +203,7 @@
                 whole((modes, 2, N, N)),
                 whole((2, N, N)),
             ],
-            out_specs=[whole((blocks, N, N)), whole((modes, 2, N, N)), whole((N, N))],
+            out_specs=[whole((blocks, N + TAIL, N)), whole((2 * modes + 1, N, N))],
             scratch_shapes=[
                 pltpu.VMEM((modes, 2, N, N), F32),
                 pltpu.VMEM((modes, 2, N, N), F32),
@@ -190,9 +213,8 @@
             ],
         ),
         out_shape=[
-            jax.ShapeDtypeStruct((blocks, N, N), F32),
-            jax.ShapeDtypeStruct((modes, 2, N, N), F32),
-            jax.ShapeDtypeStruct((N, N), F32),
+            jax.ShapeDtypeStruct((blocks, N + TAIL, N), I16),
+            jax.ShapeDtypeStruct((2 * modes + 1, N, N), F32),
         ],
         compiler_params=pltpu.CompilerParams(vmem_limit_bytes=60 * 2**20),
         name="project",
@@ -265,39 +287,271 @@
     )(place, pos_own, pos_above, probe)
 
 
-def gather_kernel_sum(place, pos, received, out):
-    pair = place[0] // 2
-    rows, cols = iota(0), iota(1)
-    out[...] = jnp.zeros_like(out)
-    per_device = pos.shape[0] // received.shape[0]
-
-    @pl.loop(0, pos.shape[0])
-    def _(k):
-        owner = pos[k, 1] // N
-        row_shift, col_shift = pos[k, 0] % N, pos[k, 1] % N
+def finish_kernel(
+    pos,
+    slots,
+    sums,
+    probe,
+    field,
+    cover,
+    object_out,
+    probe_out,
+    received,
+    core_in,
+    x_out,
+    x_in,
+    y_part,
+    y_in,
+    z_in,
+    coded,
+    acc,
+    spill_in,
+    swap_in,
+    tail_in,
+    send_sem,
+    recv_sem,
+):
+    scan_count, tile_count = lax.axis_size("scan"), lax.axis_size("tile")
+    me, tile = lax.axis_index("scan"), lax.axis_index("tile")
+    x, core = tile // 2, tile % 2
+    y, z = me // 4, me % 4
+    planes = sums.shape[0]
+    pair, parity = me // 2, me % 2
+    per_device = pos.shape[0] // scan_count
+    CORE, XR, YR, ZR, YG, XG, CG, SP, SW, TL = 16, 17, 20, 23, 27, 31, 35, 39, 40, 41
+
+    def copy(src, dst, send, recv, scan=None, tile_to=None):
+        where = {"scan": me if scan is None else scan, "tile": tile if tile_to is None else tile_to}
+        return pltpu.make_async_remote_copy(
+            src_ref=src,
+            dst_ref=dst,
+            send_sem=send_sem.at[send],
+            recv_sem=recv_sem.at[recv],
+            device_id=where,
+            device_id_type=MESH,
+        )
+
+    barrier = pltpu.get_barrier_semaphore()
+
+    @pl.loop(1, scan_count)
+    def _(d):
+        pl.semaphore_signal(barrier, 1, device_id={"scan": (me + d) % scan_count, "tile": tile}, device_id_type=MESH)
+
+    @pl.loop(1, tile_count)
+    def _(d):
+        pl.semaphore_signal(barrier, 1, device_id={"scan": me, "tile": (tile + d) % tile_count}, device_id_type=MESH)
+
+    pl.semaphore_wait(barrier, scan_count + tile_count - 2)
+
+    partner = tile + 1 - 2 * core
+    other_lanes = pl.ds(pl.multiple_of((1 - core) * H, H), H)
+    own_lanes = pl.ds(pl.multiple_of(core * H, H), H)
+    core_copy = copy(sums.at[:, :, other_lanes], core_in, CORE, CORE, tile_to=partner)
+    core_copy.start()
+
+    def update_copy(d):
+        to = (me + d) % scan_count
+        return copy(slots.at[to], received.at[d], d, d, scan=to)
+
+    @pl.loop(1, scan_count)
+    def _(d):
+        update_copy(d).start()
+
+    acc[...] = jnp.zeros_like(acc)
+
+    def collect(source, ref):
+        owner, row_shift, col_shift = jnp.int32(-4), jnp.int32(0), jnp.int32(0)
+        for k in range(per_device):
+            spot_row, spot_col = pos[source * per_device + k, 0], pos[source * per_device + k, 1]
+            hit = spot_col // (2 * N) == pair
+            owner = jnp.where(hit, spot_col // N, owner)
+            row_shift = jnp.where(hit, spot_row % N, row_shift)
+            col_shift = jnp.where(hit, spot_col % N, col_shift)
         side = owner - 2 * pair
-
-        @pl.when((side == 0) | (side == 1))
-        def _():
-            value = received[k // per_device]
-            low, right = rows < row_shift, cols >= col_shift
-            out[0, side] += jnp.where(low, 0.0, jnp.where(right, value, 0.0))
-            out[0, side + 1] += jnp.where(low, 0.0, jnp.where(right, 0.0, value))
-            out[1, side] += jnp.where(low, jnp.where(right, value, 0.0), 0.0)
-            out[1, side + 1] += jnp.where(low, jnp.where(right, 0.0, value), 0.0)
-
-
-def collect(place, pos, received):
-    whole = lambda shape: pl.BlockSpec(shape, lambda i, *_: (0,) * len(shape))
+        cols = lax.broadcasted_iota(jnp.int32, (32, N), 1)
+        right = cols >= col_shift
+        head = jnp.broadcast_to(side, (32, N)) == 0
+        tail = jnp.broadcast_to(side, (32, N)) == 1
+        picks = (head & right, (head & ~right) | (tail & right), tail & ~right)
+        scale = decode_scale(ref[N:])
+
+        for part in range(0, N, 32):
+            rows = lax.broadcasted_iota(jnp.int32, (32, N), 0) + part
+            value = decode(ref[part : part + 32], scale)
+            low = rows < row_shift
+            for block in range(3):
+                taken = jnp.where(picks[block], value, 0.0)
+                acc[0, block, part : part + 32] += jnp.where(low, 0.0, taken)
+                acc[1, block, part : part + 32] += jnp.where(low, taken, 0.0)
+
+    def collect_far(d, carry):
+        update_copy(d).wait_recv()
+        collect((me + scan_count - d) % scan_count, received.at[d])
+        return carry
+
+    collect(me, slots.at[me])
+
+    core_copy.wait_recv()
+    x_copies = []
+    for d in range(1, 4):
+        to = (x + d) % 4
+        rows = pl.ds(pl.multiple_of(to * 64, 64), 64)
+        chunk = sums[:, rows, own_lanes] + core_in[:, rows]
+        code, tail = encode(chunk.reshape(planes * 64, H))
+        x_out[d - 1, : planes * 64] = code
+        x_out[d - 1, planes * 64 :] = tail
+        x_copies.append(copy(x_out.at[d - 1], x_in.at[d - 1], XR + d - 1, XR + d - 1, tile_to=2 * to + core))
+        x_copies[-1].start()
+    rows = pl.ds(pl.multiple_of(x * 64, 64), 64)
+    y_part[...] = sums[:, rows, own_lanes] + core_in[:, rows]
+
+    lax.fori_loop(1, 8, collect_far, 0)
+
+    for d in range(1, 4):
+        x_copies[d - 1].wait_recv()
+        scale = decode_scale(x_in[d - 1, planes * 64 :])
+        y_part[...] += decode(x_in[d - 1, : planes * 64], scale).reshape(planes, 64, H)
+    y_copies = []
+    for d in range(1, 4):
+        to = (y + d) % 4
+        rows = pl.ds(pl.multiple_of(to * 16, 16), 16)
+        y_copies.append(copy(y_part.at[:, rows], y_in.at[d - 1], YR + d - 1, YR + d - 1, scan=4 * to + z))
+        y_copies[-1].start()
+
+    lax.fori_loop(8, scan_count, collect_far, 0)
+    below_tile = (tile + 1) % tile_count
+    spill_copy = copy(acc.at[1], spill_in, SP, SP, tile_to=below_tile)
+    spill_copy.start()
+
+    rows = pl.ds(pl.multiple_of(y * 16, 16), 16)
+    chunk = y_part[:, rows]
+    for d in range(1, 4):
+        y_copies[d - 1].wait_recv()
+        chunk = chunk + y_in[d - 1]
+    z_in[z] = chunk
+    z_copies = []
+    for d in range(1, 4):
+        to = (z + d) % 4
+        z_copies.append(copy(z_in.at[z], z_in.at[z], ZR + d, ZR + d, scan=4 * y + to))
+        z_copies[-1].start()
+
+    spill_copy.wait_recv()
+    acc[0] += spill_in[...]
+    swap_copy = copy(acc.at[0, 1 - parity], swap_in, SW, SW, scan=me + 1 - 2 * parity)
+    swap_copy.start()
+    tail_copy = copy(
+        acc.at[0, 2], tail_in.at[parity], TL, TL + parity, scan=(me + 2 - parity) % scan_count
+    )
+    tail_copy.start()
+
+    for d in range(1, 4):
+        source = (z + 4 - d) % 4
+        copy(z_in.at[source], z_in.at[source], ZR + d, ZR + d, scan=4 * y + source).wait_recv()
+    total = z_in[0] + z_in[1] + z_in[2] + z_in[3]
+    rows = pl.ds(pl.multiple_of(x * 64 + y * 16, 16), 16)
+    old = probe[:, rows, own_lanes]
+    fresh = (old + total[: planes - 1]) / (1.0 + total[planes - 1 :])
+    code, tail = encode(fresh.reshape((planes - 1) * 16, H))
+    spot = core * 16 + x * 4 + y
+    coded[spot, : (planes - 1) * 16] = code
+    coded[spot, (planes - 1) * 16 :] = tail
+
+    yg_copies = []
+    for d in range(1, 4):
+        yg_copies.append(copy(coded.at[spot], coded.at[spot], YG + d, YG + d, scan=4 * ((y + d) % 4) + z))
+        yg_copies[-1].start()
+    for d in range(1, 4):
+        source = core * 16 + x * 4 + (y + 4 - d) % 4
+        copy(coded.at[source], coded.at[source], YG + d, YG + d, scan=4 * ((y + d) % 4) + z).wait_recv()
+
+    group = pl.ds(core * 16 + x * 4, 4)
+    xg_copies = []
+    for d in range(1, 4):
+        to = 2 * ((x + d) % 4) + core
+        xg_copies.append(copy(coded.at[group], coded.at[group], XG + d, XG + d, tile_to=to))
+        xg_copies[-1].start()
+    cg_copies = [copy(coded.at[group], coded.at[group], CG, CG, tile_to=partner)]
+    cg_copies[-1].start()
+
+    swap_copy.wait_recv()
+
+    @pl.when(parity == 0)
+    def _():
+        for plane in range(2):
+            copy(acc.at[0, 2], tail_in.at[plane], TL, TL + plane, scan=(me + 2) % scan_count).wait_recv()
+        share = 1.0 / (1.0 + cover[...])
+        object_out[0] = (field[0] + (acc[0, 0] + tail_in[0])) * share
+        object_out[1] = (field[1] + (swap_in[...] + tail_in[1])) * share
+
+    @pl.when(parity == 1)
+    def _():
+        share = 1.0 / (1.0 + cover[...])
+        object_out[0] = (field[0] + swap_in[...]) * share
+        object_out[1] = (field[1] + acc[0, 1]) * share
+
+    def show(core_at, x_at):
+        for y_at in range(4):
+            at = core_at * 16 + x_at * 4 + y_at
+            scale = decode_scale(coded[at, (planes - 1) * 16 :])
+            value = decode(coded[at, : (planes - 1) * 16], scale).reshape(planes - 1, 16, H)
+            rows = pl.ds(pl.multiple_of(x_at * 64 + y_at * 16, 16), 16)
+            lanes = pl.ds(pl.multiple_of(core_at * H, H), H)
+            probe_out[:, rows, lanes] = value
+
+    show(core, x)
+    for d in range(1, 4):
+        source = (x + 4 - d) % 4
+        at = pl.ds(core * 16 + source * 4, 4)
+        copy(coded.at[at], coded.at[at], XG + d, XG + d, tile_to=2 * source + core).wait_recv()
+        cg_copies.append(copy(coded.at[at], coded.at[at], CG + d, CG + d, tile_to=partner))
+        cg_copies[-1].start()
+        show(core, source)
+    for d in range(4):
+        source = (x + 4 - d) % 4
+        at = pl.ds((1 - core) * 16 + source * 4, 4)
+        copy(coded.at[at], coded.at[at], CG + d, CG + d, tile_to=partner).wait_recv()
+        show(1 - core, source)
+
+    @pl.loop(1, scan_count)
+    def _(d):
+        update_copy(d).wait_send()
+
+    for started in [core_copy, spill_copy, swap_copy, tail_copy] + x_copies + y_copies + z_copies:
+        started.wait_send()
+    for started in yg_copies + xg_copies + cg_copies:
+        started.wait_send()
+
+
+def finish(pos, slots, sums, probe, field, cover):
+    scan_count = slots.shape[0]
+    planes = sums.shape[0]
+    vmem = pl.BlockSpec(memory_space=pltpu.VMEM)
     return pl.pallas_call(
-        gather_kernel_sum,
-        grid_spec=pltpu.PrefetchScalarGridSpec(
-            num_scalar_prefetch=2, grid=(1,), in_specs=[whole(received.shape)], out_specs=whole((2, 3, N, N))
+        finish_kernel,
+        in_specs=[pl.BlockSpec(memory_space=pltpu.SMEM)] + [vmem] * 5,
+        out_specs=[vmem, vmem],
+        out_shape=[jax.ShapeDtypeStruct(field.shape, F32), jax.ShapeDtypeStruct(probe.shape, F32)],
+        scratch_shapes=[
+            pltpu.VMEM((scan_count, N + TAIL, N), I16),
+            pltpu.VMEM((planes, N, H), F32),
+            pltpu.VMEM((3, planes * 64 + TAIL, H), I16),
+            pltpu.VMEM((3, planes * 64 + TAIL, H), I16),
+            pltpu.VMEM((planes, 64, H), F32),
+            pltpu.VMEM((3, planes, 16, H), F32),
+            pltpu.VMEM((4, planes, 16, H), F32),
+            pltpu.VMEM((32, (planes - 1) * 16 + TAIL, H), I16),
+            pltpu.VMEM((2, 3, N, N), F32),
+            pltpu.VMEM((3, N, N), F32),
+            pltpu.VMEM((N, N), F32),
+            pltpu.VMEM((2, N, N), F32),
+            pltpu.SemaphoreType.DMA((44,)),
+            pltpu.SemaphoreType.DMA((44,)),
+        ],
+        compiler_params=pltpu.CompilerParams(
+            collective_id=1, has_side_effects=True, vmem_limit_bytes=56 * 2**20
         ),
-        out_shape=jax.ShapeDtypeStruct((2, 3, N, N), F32),
-        compiler_params=pltpu.CompilerParams(vmem_limit_bytes=40 * 2**20),
-        name="collect",
-    )(place, pos, received)
+        name="finish",
+    )(pos, slots, sums, probe, field, cover)
 
 
 def shifted(value, axis, steps):
@@ -320,21 +574,11 @@
     pos_above = pos_above.reshape(-1, 2)
     band = lax.all_gather(object_field.astype(BF16), "scan", axis=0, tiled=False)
     below = shifted(cut(pos_prev, band), "tile", -1)
-    slots, numer, denom = project(positions, band, below, patterns, probe_modes, table)
-    received = lax.all_to_all(slots, "scan", split_axis=0, concat_axis=0, tiled=True)
+    slots, sums = project(positions, band, below, patterns, probe_modes, table)
     cover = cover_of(place, pos_own, pos_above, probe_modes)
-    numer, denom = lax.psum((numer, denom), ("scan", "tile"))
-    sums = collect(place, pos_own, received)
-    sums = sums[0] + shifted(sums[1], "tile", 1)
-    odd = me % 2 == 1
-    swapped = lax.ppermute(jnp.where(odd, sums[0], sums[1]), "scan", [(s, s ^ 1) for s in range(scan_count)])
-    tail_re = lax.ppermute(sums[2], "scan", [(s, (s + 2) % scan_count) for s in range(0, scan_count, 2)])
-    tail_im = lax.ppermute(sums[2], "scan", [(s, (s + 1) % scan_count) for s in range(1, scan_count, 2)])
-    whole_re = jnp.where(odd, swapped, sums[0] + tail_re)
-    whole_im = jnp.where(odd, sums[1], swapped + tail_im)
-    object_now = (object_field + jnp.stack([whole_re, whole_im])) / (1.0 + cover)
-    probe_now = (probe_modes + numer) / (1.0 + denom)
-    return (object_now, probe_now)
+    flat_probe = probe_modes.reshape(-1, N, N)
+    object_now, probe_now = finish(pos_own, slots, sums, flat_probe, object_field, cover)
+    return (object_now, probe_now.reshape(probe_modes.shape))
 
 
 def solution(mesh):

time: 378 us -> 271 us (0.72)
  waiting for transfers between devices: 213 us -> 17.4 us
  Pallas kernels: 79.8 us -> 183 us
  starting transfers between devices: 17.3 us -> 0.71 us
  other arithmetic: 8.95 us -> 1.85 us
  local copies, waits for them, and re-layouts: 5.27 us -> 12.2 us
    psum x1 -> x0, waiting for transfers between devices: 118 us -> none  [body(): numer, denom = lax.psum((numer, denom), ('scan', 'tile'))]
    pallas_call x1, Pallas kernels: 5.72 us -> 105 us  [finish(): pl.pallas_call(finish_kernel, in_specs=[pl.BlockSpec(memory_space=pltpu.S...]
    all_to_all x1 -> x0, waiting for transfers between devices: 56.4 us -> none  [body(): lax.all_to_all(slots, 'scan', split_axis=0, concat_axis=0, tiled=True)]
    ppermute x2 -> x1, waiting for transfers between devices: 13.1 us -> 0.13 us  [shifted(): lax.ppermute(value, axis, [(s, (s + steps) % count) for s in range(count)])]
    unnamed x11 -> x13, local copies, waits for them, and re-layouts: 4.08 us -> 11.1 us
    ppermute x3 -> x0, waiting for transfers between devices: 6.88 us -> none  [the longest x1 3.69 us: body(): lax.ppermute(jnp.where(odd, sums[0], sums[1]), 'scan', [(s, s ^ 1) for s...]
    ppermute x3 -> x0, starting transfers between devices: 6.59 us -> none  [the longest x1 4.34 us: body(): lax.ppermute(sums[2], 'scan', [(s, (s + 2) % scan_count) for s in range(0...]
    div x2 -> x0, other arithmetic: 5.75 us -> none  [the longest x1 4.87 us: body(): probe_now = (probe_modes + numer) / (1.0 + denom)]
  transfers between devices with their start and end apart: 8 -> 2, of which waited for: 6 -> 2; matrix products, arithmetic and copies ran while one was open for 2% -> 1% of each run, Pallas kernels for 4% -> 4%
where the time goes in v2:
time: 271 us; the launch traced here: 268 us
  Pallas kernels  183 us (68%)
  blocking collectives  38.7 us (14%)
  waiting for transfers between devices  17.4 us (6%)
  between operations  14.1 us (5%)
  local copies, waits for them, and re-layouts  12.2 us (5%)
    pallas_call x1, Pallas kernels, finish(): pl.pallas_call(finish_kernel, in_specs=[pl.BlockSpec(memory_space=pltpu.S...  105 us
    pallas_call x1, Pallas kernels, project(): pl.pallas_call(project_kernel, grid_spec=pltpu.PrefetchScalarGridSpec(num...  64 us
    all_gather x1, blocking collectives, body(): pos_all = lax.all_gather(positions, ('scan', 'tile'), axis=0, tiled=True)  38.7 us
    all_gather x1, waiting for transfers between devices, body(): lax.all_gather(object_field.astype(BF16), 'scan', axis=0, tiled=False)  17.3 us
    unnamed x13, local copies, waits for them, and re-layouts  11.1 us
    pallas_call x1, Pallas kernels, cover_of(): pl.pallas_call(cover_kernel, grid_spec=pltpu.PrefetchScalarGridSpec(num_s...  9.55 us
  transfers between devices with their start and end apart: 2, of which 2 were waited for; matrix products, arithmetic and copies ran while one was open for 1% of the time, Pallas kernels for 4%

profile of v2, /device:TPU:1, one launch (start us, length us, event | category | flops | bytes accessed | tf_op | source)
XLA Modules:
  0.0 268.1 jit_solution(17878751295809051475)
XLA Ops:
  7.2 0.0 all-gather.4.cloned.1.call-start
  7.2 1.8 convert_element_type.3
  9.0 0.0 all-gather.4.cloned.1.call-update
  9.0 38.7 %all-gather.1 = s32[128,4,2]{1,2,0:T(2,128)S(1)} all-gather(s32[1,4,2]{1,2,0:T(2,128)} %bitcast.21), channel_id=1, replica_groups=mesh['scan'=16,'tile'=8] {'scan','tile'}, dimensions={0}, use_global_device_ids=true | all-gather | bytes 4128 | tf_op jit(solution)/shard_map/all_gather | solution.py:567
  47.7 0.7 copy.22.pos
  48.4 17.3 %all-gather.4.cloned.1.call-done = bf16[32,256,256]{2,1,0:T(8,128)(2,1)} async-done(((bf16[2,256,256]{2,1,0:T(8,128)(2,1)}), bf16[32,256,256]{2,1,0:T(8,128)(2,1)}) %all-gather.4.cloned.1.call-update) | async-done | bytes 4194320 | tf_op jit(solution)/shard_map/all_gather | solution.py:575
  65.7 0.0 copy-start.4
  65.7 4.5 %cut.1 = bf16[4,2,256,256]{3,2,1,0:T(8,128)(2,1)} custom-call(s32[4,2]{1,0:T(4,128)} %copy.22.pos, bf16[16,2,256,256]{3,2,1,0:T(8,128)(2,1)} %bitcast.14, bf16[16,2,256,256]{3,2,1,0:T(8,128)(2,1)} %bitcast.15), custom_call_target="tpu_custom_call" | custom-call | tf_op jit(solution)/shard_map/cut/pallas_call | solution.py:236
  70.2 0.7 collective-permute-start
  70.9 0.0 copy-done.4
  70.9 0.7 copy.23.pos
  71.5 0.2 copy.28
  71.8 0.0 copy-start.2
  71.8 0.2 copy.30
  72.0 0.1 pad_add_fusion.place
  72.0 0.0 copy-start
  72.0 2.2 copy-done
  74.2 9.6 %cover.1 = f32[256,256]{1,0:T(8,128)S(1)} custom-call(s32[2]{0:T(128)S(1)} %pad_add_fusion.place, s32[64,2]{1,0:T(8,128)S(1)} %bitcast.11, s32[64,2]{1,0:T(8,128)S(1)} %bitcast.13, f32[8,2,256,256]{3,2,1,0:T(8,128)S(1)} %copy-done), custom_call_target="tpu_custom_call" | custom-call | tf_op jit(solution)/shard_map/cover/pallas_call | solution.py:279
  83.8 0.0 copy-start.1
  83.8 0.7 copy-done.1
  84.5 0.1 collective-permute-done.below
  84.6 0.0 copy-start.3
  84.6 1.1 copy-done.3
  85.7 64.0 %project.1 = (s16[16,272,256]{2,1,0:T(8,128)(2,1)}, f32[17,256,256]{2,1,0:T(8,128)}) custom-call(s32[4,2]{1,0:T(4,128)} %copy.23.pos, bf16[16,2,256,256]{3,2,1,0:T(8,128)(2,1)} %bitcast.16, bf16[16,2,256,256]{3,2,1,0:T(8,128)(2,1)} %bitcast.17, bf16[4,2,256,256]{3,2,1,0:T(8,128)(2,1)} %copy-done.3, f32[4,256,256]{2,1,0:T(8,128)} %pattern.1, ...), custom_call_target="tpu_custom_call" | custom-call | tf_op jit(solution)/shard_map/project/pallas_call | solution.py:193
  149.7 0.0 copy-done.2
  149.7 105.1 %finish.1 = (f32[2,256,256]{2,1,0:T(8,128)}, f32[16,256,256]{2,1,0:T(8,128)}) custom-call(s32[64,2]{1,0:T(8,128)} %bitcast.12, s16[16,272,256]{2,1,0:T(8,128)(2,1)} %get-tuple-element.6.slots, f32[17,256,256]{2,1,0:T(8,128)} %get-tuple-element.7.sums, f32[16,256,256]{2,1,0:T(8,128)} %bitcast.10, f32[2,256,256]{2,1,0:T(8,128)} %field.1, f32[256,256]{1,0:T(8,128)} %copy-done.1), custom_call_target="tpu_custom_call" | custom-call | tf_op jit(solution)/shard_map/finish/pallas_call | solution.py:529
  254.8 1.9 copy.35
  256.7 4.6 %copy.36 = f32[8,2,256,256]{3,2,1,0:T(8,128)} copy(f32[8,2,256,256]{3,2,1,0:T(8,128)} %bitcast.18) | data formatting | bytes 8388608
  (2 shorter events, 0.0 us)
Async XLA Ops:
  7.2 58.5 %all-gather.4.cloned.1.call-start = ((), (), s32[]{:S(2)}) async-start(), calls=%async_computation | async-start | bytes 4456448 | tf_op jit(solution)/shard_map/all_gather | solution.py:575
  65.7 5.2 %copy-start.4 = (s32[4,2]{0,1:T(2,128)S(1)}, s32[4,2]{0,1:T(2,128)}, u32[]{:S(2)}) copy-start(s32[4,2]{0,1:T(2,128)} %param.8) | copy-start | bytes 100
  70.2 14.4 %collective-permute-start = (bf16[4,2,256,256]{3,2,1,0:T(8,128)(2,1)}, bf16[4,2,256,256]{3,2,1,0:T(8,128)(2,1)S(1)}, u32[]{:S(2)}, u32[]{:S(2)}) collective-permute-start(bf16[4,2,256,256]{3,2,1,0:T(8,128)(2,1)} %cut.1), channel_id=1, source_target_pairs={{0,7},{1,0},{2,1},{3,2},{4,3},{5,4},{6,5},{7,6},{8,15},{9,8},{10,9... | collective-permute-start | bytes 3145736 | tf_op jit(solution)/shard_map/ppermute | solution.py:559
  71.8 78.0 %copy-start.2 = (s32[16,1,4,2]{3,2,0,1:T(4,128)}, s32[16,1,4,2]{3,2,0,1:T(4,128)S(1)}, u32[]{:S(2)}) copy-start(s32[16,1,4,2]{3,2,0,1:T(4,128)S(1)} %copy.28) | copy-start | bytes 1540
  72.0 2.2 copy-start
  83.8 0.7 copy-start.1
  84.6 1.1 copy-start.3
Sparse Core Ops, SparseCore 0:
  10.7 54.9 all-gather.3

commit v3 on v2

--- a/solution.py
+++ b/solution.py
@@ -114,10 +114,10 @@
 
 
 def project_kernel(
-    pos, near, far_block, below, pattern, probe, table, slots, sums, folded_probe, far, power, patch, update
+    pos, near, far_block, below, level, folded_probe, table, slots, sums, far, power, patch, update
 ):
     step = pl.program_id(0)
-    modes = probe.shape[0]
+    modes = folded_probe.shape[0] // 2
     row_shift, col_shift = pos[step, 0] % N, pos[step, 1] % N
     pair = pos[step, 1] // (2 * N)
     rows, cols = iota(0), iota(1)
@@ -127,11 +127,6 @@
     def _():
         slots[...] = jnp.zeros_like(slots)
         sums[...] = jnp.zeros_like(sums)
-
-        @pl.loop(0, modes)
-        def _(m):
-            for plane in range(2):
-                folded_probe[m, plane] = permute(probe[m, plane], fold_matrix, fold_matrix, 3)
 
     row_pick = one_hot(cols == (row_shift + folded(rows)) % N)
     row_back = one_hot(rows == (row_shift + folded(cols)) % N)
@@ -145,7 +140,7 @@
 
     @pl.loop(0, modes)
     def _(m):
-        p_re, p_im = folded_probe[m, 0], folded_probe[m, 1]
+        p_re, p_im = folded_probe[2 * m], folded_probe[2 * m + 1]
         o_re, o_im = patch[0], patch[1]
         wave_re = (p_re * o_re - p_im * o_im).astype(BF16)
         wave_im = (p_re * o_im + p_im * o_re).astype(BF16)
@@ -154,8 +149,7 @@
         far[m, 1] = f_im
         power[...] += f_re * f_re + f_im * f_im
 
-    level = permute(pattern[0], fold_matrix, fold_matrix, 3)
-    power[...] = jnp.sqrt(level) / jnp.sqrt(power[...])
+    power[...] = level[0] / jnp.sqrt(power[...])
     update[...] = jnp.zeros_like(update)
 
     @pl.loop(0, modes)
@@ -164,7 +158,7 @@
         fixed_re = (far[m, 0] * scaling).astype(BF16)
         fixed_im = (far[m, 1] * scaling).astype(BF16)
         e_re, e_im = transform(fixed_re, fixed_im, table, 1.0)
-        p_re, p_im = folded_probe[m, 0], folded_probe[m, 1]
+        p_re, p_im = folded_probe[2 * m], folded_probe[2 * m + 1]
         update[0] += p_re * e_re + p_im * e_im
         update[1] += p_re * e_im - p_im * e_re
         o_re, o_im = patch[0], patch[1]
@@ -184,8 +178,8 @@
             sums[m] = permute(sums[m], fold_matrix, fold_matrix, 2)
 
 
-def project(positions, band, below, patterns, probe, table):
-    count, (modes,) = patterns.shape[0], probe.shape[:1]
+def project(positions, band, below, level, folded_probe, table):
+    count, modes = level.shape[0], folded_probe.shape[0] // 2
     blocks = band.shape[0]
     whole = lambda shape: pl.BlockSpec(shape, lambda k, pos: (0,) * len(shape))
     near = pl.BlockSpec((1, 2, N, N), lambda k, pos: (pos[k, 1] // N, 0, 0, 0))
@@ -200,12 +194,11 @@
                 after,
                 pl.BlockSpec((1, 2, N, N), lambda k, pos: (k, 0, 0, 0)),
                 pl.BlockSpec((1, N, N), lambda k, pos: (k, 0, 0)),
-                whole((modes, 2, N, N)),
+                whole((2 * modes, N, N)),
                 whole((2, N, N)),
             ],
             out_specs=[whole((blocks, N + TAIL, N)), whole((2 * modes + 1, N, N))],
             scratch_shapes=[
-                pltpu.VMEM((modes, 2, N, N), F32),
                 pltpu.VMEM((modes, 2, N, N), F32),
                 pltpu.VMEM((N, N), F32),
                 pltpu.VMEM((2, N, N), F32),
@@ -218,73 +211,237 @@
         ],
         compiler_params=pltpu.CompilerParams(vmem_limit_bytes=60 * 2**20),
         name="project",
-    )(positions, band, band, below, patterns, probe, table)
-
-
-def cut_kernel(pos, near, after, out):
-    step = pl.program_id(0)
-    col_shift = pos[step, 1] % N
-    cols = iota(1)
-    for plane in range(2):
-        out[0, plane] = jnp.where(
-            cols >= col_shift, near[0, plane].astype(F32), after[0, plane].astype(F32)
-        ).astype(BF16)
-
-
-def cut(positions, band):
-    count, blocks = positions.shape[0], band.shape[0]
+    )(positions, band, band, below, level, folded_probe, table)
+
+
+def remote(src, dst, send, recv, scan, tile):
+    return pltpu.make_async_remote_copy(
+        src_ref=src,
+        dst_ref=dst,
+        send_sem=send,
+        recv_sem=recv,
+        device_id={"scan": scan, "tile": tile},
+        device_id_type=MESH,
+    )
+
+
+def greet():
+    scan_count, tile_count = lax.axis_size("scan"), lax.axis_size("tile")
+    me, tile = lax.axis_index("scan"), lax.axis_index("tile")
+    barrier = pltpu.get_barrier_semaphore()
+
+    @pl.loop(1, scan_count)
+    def _(d):
+        pl.semaphore_signal(barrier, 1, device_id={"scan": (me + d) % scan_count, "tile": tile}, device_id_type=MESH)
+
+    @pl.loop(1, tile_count)
+    def _(d):
+        pl.semaphore_signal(barrier, 1, device_id={"scan": me, "tile": (tile + d) % tile_count}, device_id_type=MESH)
+
+    pl.semaphore_wait(barrier, scan_count + tile_count - 2)
+
+
+def gather_kernel(
+    block,
+    spots,
+    probe,
+    patterns,
+    band,
+    below,
+    spots_own,
+    cover,
+    folded_probe,
+    level,
+    cut,
+    spots_above,
+    spot_words,
+    spot_words_above,
+    power,
+    send_sem,
+    recv_sem,
+    spot_send,
+    spot_recv,
+    cut_send,
+    cut_recv,
+    local_sem,
+):
+    scan_count, tile_count = lax.axis_size("scan"), lax.axis_size("tile")
+    me, tile = lax.axis_index("scan"), lax.axis_index("tile")
+    y, z = me // 4, me % 4
+    next_tile, last_tile = (tile + 1) % tile_count, (tile + tile_count - 1) % tile_count
+    per_device = patterns.shape[0]
+    greet()
+
+    def spot_copy(d):
+        return remote(
+            spots, spots_own.at[me], spot_send.at[d], spot_recv.at[d], (me + d) % scan_count, tile
+        )
+
+    @pl.loop(1, scan_count)
+    def _(d):
+        spot_copy(d).start()
+
+    def along(plane, stage, d):
+        turn_z = (plane == 0) == (stage == 0)
+        return 4 * y + (z + d) % 4 if turn_z else 4 * ((y + d) % 4) + z
+
+    sent = []
+
+    def push(src, source, plane, stage, d):
+        move = remote(
+            src,
+            band.at[source, plane],
+            send_sem.at[len(sent)],
+            recv_sem.at[2 * source + plane],
+            along(plane, stage, d),
+            tile,
+        )
+        move.start()
+        sent.append(move)
+
+    for stage in range(2):
+        for d in (1, 3, 2):
+            for plane in range(2):
+                push(block.at[plane], me, plane, stage, d)
+
+    def landed(source, plane):
+        remote(block.at[plane], band.at[source, plane], send_sem.at[0], recv_sem.at[2 * source + plane], along(0, 0, 1), tile).wait_recv()
+
+    spots_own[me] = spots[...]
+    band[me] = block[...]
+    total = jnp.zeros((N, N), F32)
+    for plane in range(probe.shape[0]):
+        total = total + probe[plane] * probe[plane]
+    power[...] = total
+
+    for d in (3, 1, 2):
+        for plane in range(2):
+            source = along(plane, 0, d)
+            landed(source, plane)
+            for turn in (1, 3, 2):
+                push(band.at[source, plane], source, plane, 1, turn)
+
+    @pl.loop(1, scan_count)
+    def _(d):
+        source = (me + scan_count - d) % scan_count
+        remote(spots, spots_own.at[source], spot_send.at[d], spot_recv.at[d], source, tile).wait_recv()
+
+    above_copy = remote(spots_own, spots_above, spot_send.at[0], spot_recv.at[0], me, next_tile)
+    above_copy.start()
+    words_copy = pltpu.make_async_copy(spots_own, spot_words, local_sem.at[0])
+    words_copy.start()
+
+    fold_matrix = one_hot(iota(0) == folded(iota(1)))
+
+    @pl.loop(0, probe.shape[0])
+    def _(plane):
+        folded_probe[plane] = permute(probe[plane], fold_matrix, fold_matrix, 3)
+
+    @pl.loop(0, per_device)
+    def _(k):
+        level[k] = jnp.sqrt(permute(patterns[k], fold_matrix, fold_matrix, 3))
+
+    cover[...] = jnp.zeros_like(cover)
+
+    def add_cover(words, above):
+        @pl.loop(0, scan_count)
+        def _(source):
+            head, row_shift, col_shift = jnp.int32(-1), jnp.int32(0), jnp.int32(0)
+            for k in range(per_device):
+                row, col = words[source, 0, 2 * k], words[source, 0, 2 * k + 1]
+                owner = col // N
+                first = owner == me
+                hit = first | ((owner + 1) % scan_count == me)
+                head = jnp.where(hit, first.astype(jnp.int32), head)
+                row_shift = jnp.where(hit, row % N, row_shift)
+                col_shift = jnp.where(hit, col % N, col_shift)
+            start = jnp.where(head == 1, col_shift, 0)
+            stop = jnp.where(head == 1, N, jnp.where(head == 0, col_shift, 0))
+            rows, cols = iota(0), iota(1)
+            moved = pltpu.roll(pltpu.roll(power[...], row_shift, 0), col_shift, 1)
+            keep = (rows < row_shift) if above else (rows >= row_shift)
+            cover[...] += jnp.where(keep & (cols >= start) & (cols < stop), moved, 0.0)
+
+    words_copy.wait()
+    add_cover(spot_words, False)
+    above_copy.wait_recv()
+    words_copy = pltpu.make_async_copy(spots_above, spot_words_above, local_sem.at[1])
+    words_copy.start()
+    words_copy.wait()
+    add_cover(spot_words_above, True)
+
+    for d in (3, 1, 2):
+        for plane in range(2):
+            for turn in (3, 1, 2):
+                if plane == 0:
+                    source = 4 * ((y + turn) % 4) + (z + d) % 4
+                else:
+                    source = 4 * ((y + d) % 4) + (z + turn) % 4
+                landed(source, plane)
+    for turn in (3, 1, 2):
+        landed(4 * ((y + turn) % 4) + z, 0)
+        landed(4 * y + (z + turn) % 4, 1)
+
+    cuts = []
+    cols = lax.broadcasted_iota(jnp.int32, (N, N), 1)
+    for k in range(per_device):
+        col = spot_words_above[me, 0, 2 * k + 1]
+        owner, col_shift = col // N, col % N
+        after = (owner + 1) % scan_count
+        for plane in range(2):
+            cut[k, plane] = jnp.where(
+                cols >= col_shift, band[owner, plane].astype(F32), band[after, plane].astype(F32)
+            ).astype(BF16)
+        cuts.append(remote(cut.at[k], below.at[k], cut_send.at[k], cut_recv.at[k], me, last_tile))
+        cuts[-1].start()
+
+    for move in cuts:
+        move.wait()
+    for move in sent:
+        move.wait_send()
+    above_copy.wait_send()
+
+    @pl.loop(1, scan_count)
+    def _(d):
+        spot_copy(d).wait_send()
+
+
+def gather(block, spots, probe, patterns, scan_count):
+    per_device = patterns.shape[0]
+    vmem = pl.BlockSpec(memory_space=pltpu.VMEM)
+    words = (scan_count,) + spots.shape
+    dma = pltpu.SemaphoreType.DMA
     return pl.pallas_call(
-        cut_kernel,
-        grid_spec=pltpu.PrefetchScalarGridSpec(
-            num_scalar_prefetch=1,
-            grid=(count,),
-            in_specs=[
-                pl.BlockSpec((1, 2, N, N), lambda k, pos: (pos[k, 1] // N, 0, 0, 0)),
-                pl.BlockSpec((1, 2, N, N), lambda k, pos: ((pos[k, 1] // N + 1) % blocks, 0, 0, 0)),
-            ],
-            out_specs=pl.BlockSpec((1, 2, N, N), lambda k, pos: (k, 0, 0, 0)),
+        gather_kernel,
+        in_specs=[vmem] * 4,
+        out_specs=[vmem] * 6,
+        out_shape=[
+            jax.ShapeDtypeStruct((scan_count, 2, N, N), BF16),
+            jax.ShapeDtypeStruct((per_device, 2, N, N), BF16),
+            jax.ShapeDtypeStruct(words, jnp.int32),
+            jax.ShapeDtypeStruct((N, N), F32),
+            jax.ShapeDtypeStruct(probe.shape, F32),
+            jax.ShapeDtypeStruct(patterns.shape, F32),
+        ],
+        scratch_shapes=[
+            pltpu.VMEM((per_device, 2, N, N), BF16),
+            pltpu.VMEM(words, jnp.int32),
+            pltpu.SMEM(words, jnp.int32),
+            pltpu.SMEM(words, jnp.int32),
+            pltpu.VMEM((N, N), F32),
+            dma((30,)),
+            dma((2 * scan_count,)),
+            dma((scan_count,)),
+            dma((scan_count,)),
+            dma((per_device,)),
+            dma((per_device,)),
+            dma((2,)),
+        ],
+        compiler_params=pltpu.CompilerParams(
+            collective_id=0, has_side_effects=True, vmem_limit_bytes=56 * 2**20
         ),
-        out_shape=jax.ShapeDtypeStruct((count, 2, N, N), BF16),
-        name="cut",
-    )(positions, band, band)
-
-
-def cover_kernel(place, pos_own, pos_above, probe, out):
-    me, blocks = place[0], place[1]
-    rows, cols = iota(0), iota(1)
-    total = jnp.zeros((N, N), F32)
-    for m in range(probe.shape[0]):
-        total = total + (probe[m, 0] * probe[m, 0] + probe[m, 1] * probe[m, 1])
-    out[...] = jnp.zeros_like(out)
-
-    for above, pos in ((False, pos_own), (True, pos_above)):
-        @pl.loop(0, pos_own.shape[0])
-        def _(k):
-            owner = pos[k, 1] // N
-            row_shift, col_shift = pos[k, 0] % N, pos[k, 1] % N
-            head, tail = owner == me, (owner + 1) % blocks == me
-
-            @pl.when(head | tail)
-            def _():
-                moved = pltpu.roll(pltpu.roll(total, row_shift, 0), col_shift, 1)
-                keep = (rows < row_shift) if above else (rows >= row_shift)
-                split = jnp.where(head, col_shift, 0)
-                stop = jnp.where(head, N, col_shift)
-                keep = keep & (cols >= split) & (cols < stop)
-                out[...] += jnp.where(keep, moved, 0.0)
-
-
-def cover_of(place, pos_own, pos_above, probe):
-    whole = lambda shape: pl.BlockSpec(shape, lambda i, *_: (0,) * len(shape))
-    return pl.pallas_call(
-        cover_kernel,
-        grid_spec=pltpu.PrefetchScalarGridSpec(
-            num_scalar_prefetch=3, grid=(1,), in_specs=[whole(probe.shape)], out_specs=whole((N, N))
-        ),
-        out_shape=jax.ShapeDtypeStruct((N, N), F32),
-        compiler_params=pltpu.CompilerParams(vmem_limit_bytes=40 * 2**20),
-        name="cover",
-    )(place, pos_own, pos_above, probe)
+        name="gather",
+    )(block, spots, probe, patterns)
 
 
 def finish_kernel(
@@ -331,18 +488,7 @@
             device_id_type=MESH,
         )
 
-    barrier = pltpu.get_barrier_semaphore()
-
-    @pl.loop(1, scan_count)
-    def _(d):
-        pl.semaphore_signal(barrier, 1, device_id={"scan": (me + d) % scan_count, "tile": tile}, device_id_type=MESH)
-
-    @pl.loop(1, tile_count)
-    def _(d):
-        pl.semaphore_signal(barrier, 1, device_id={"scan": me, "tile": (tile + d) % tile_count}, device_id_type=MESH)
-
-    pl.semaphore_wait(barrier, scan_count + tile_count - 2)
-
+    greet()
     partner = tile + 1 - 2 * core
     other_lanes = pl.ds(pl.multiple_of((1 - core) * H, H), H)
     own_lanes = pl.ds(pl.multiple_of(core * H, H), H)
@@ -554,29 +700,16 @@
     )(pos, slots, sums, probe, field, cover)
 
 
-def shifted(value, axis, steps):
-    count = lax.axis_size(axis)
-    return lax.ppermute(value, axis, [(s, (s + steps) % count) for s in range(count)])
-
-
 def body(object_field, probe_modes, patterns, positions):
-    scan_count, tile_count = lax.axis_size("scan"), lax.axis_size("tile")
-    me, tile = lax.axis_index("scan"), lax.axis_index("tile")
+    scan_count = lax.axis_size("scan")
     table = jnp.asarray(folded_tables())
-    place = jnp.stack([me, jnp.int32(scan_count)])
-    pos_all = lax.all_gather(positions, ("scan", "tile"), axis=0, tiled=True)
-    pos_all = pos_all.reshape(scan_count, tile_count, -1, 2)
-    above_tile = (tile + tile_count - 1) % tile_count
-    pos_own = lax.dynamic_index_in_dim(pos_all, tile, 1, keepdims=False)
-    pos_above = lax.dynamic_index_in_dim(pos_all, above_tile, 1, keepdims=False)
-    pos_prev = lax.dynamic_index_in_dim(pos_above, me, 0, keepdims=False)
-    pos_own = pos_own.reshape(-1, 2)
-    pos_above = pos_above.reshape(-1, 2)
-    band = lax.all_gather(object_field.astype(BF16), "scan", axis=0, tiled=False)
-    below = shifted(cut(pos_prev, band), "tile", -1)
-    slots, sums = project(positions, band, below, patterns, probe_modes, table)
-    cover = cover_of(place, pos_own, pos_above, probe_modes)
+    spots = jnp.zeros((8, 128), jnp.int32).at[0, : positions.size].set(positions.reshape(-1))
     flat_probe = probe_modes.reshape(-1, N, N)
+    band, below, words, cover, folded_probe, level = gather(
+        object_field.astype(BF16), spots, flat_probe, patterns, scan_count
+    )
+    slots, sums = project(positions, band, below, level, folded_probe, table)
+    pos_own = words[:, 0, : positions.size].reshape(-1, 2)
     object_now, probe_now = finish(pos_own, slots, sums, flat_probe, object_field, cover)
     return (object_now, probe_now.reshape(probe_modes.shape))
 

time: 271 us -> 231 us (0.85); the launches traced: 268 us -> 231 us
  blocking collectives: 38.7 us -> 0 us
  Pallas kernels: 183 us -> 219 us
  waiting for transfers between devices: 17.4 us -> 0 us
  between operations: 14.1 us -> 0.65 us
  local copies, waits for them, and re-layouts: 12.2 us -> 9.47 us
    pallas_call x2 -> x1, Pallas kernels: 14 us -> 60.5 us  [gather(): pl.pallas_call(gather_kernel, in_specs=[vmem] * 4, out_specs=[vmem] * 6,...]
    all_gather x1 -> x0, blocking collectives: 38.7 us -> none  [body(): pos_all = lax.all_gather(positions, ('scan', 'tile'), axis=0, tiled=True)]
    all_gather x1 -> x0, waiting for transfers between devices: 17.3 us -> none  [body(): lax.all_gather(object_field.astype(BF16), 'scan', axis=0, tiled=False)]
    pallas_call x1, Pallas kernels: 64 us -> 55.1 us  [project(): pl.pallas_call(project_kernel, grid_spec=pltpu.PrefetchScalarGridSpec(num...]
    unnamed x13 -> x5, local copies, waits for them, and re-layouts: 11.1 us -> 7.23 us
  transfers between devices with their start and end apart: 2 -> 0, of which waited for: 2 -> 0; matrix products, arithmetic and copies ran while one was open for 1% -> 0% of each run, Pallas kernels for 4% -> 0%
where the time goes in v3:
time: 231 us
  Pallas kernels  219 us (95%)
  local copies, waits for them, and re-layouts  9.47 us (4%)
    pallas_call x1, Pallas kernels, finish(): pl.pallas_call(finish_kernel, in_specs=[pl.BlockSpec(memory_space=pltpu.S...  103 us
    pallas_call x1, Pallas kernels, gather(): pl.pallas_call(gather_kernel, in_specs=[vmem] * 4, out_specs=[vmem] * 6,...  60.5 us
    pallas_call x1, Pallas kernels, project(): pl.pallas_call(project_kernel, grid_spec=pltpu.PrefetchScalarGridSpec(num...  55.1 us
    unnamed x5, local copies, waits for them, and re-layouts  7.23 us

profile of v3, /device:TPU:1, one launch (start us, length us, event | category | flops | bytes accessed | tf_op | source)
XLA Modules:
  0.0 231.0 jit_solution(4441627787902263365)
XLA Ops:
  0.6 0.8 copy.9.pos
  1.4 0.0 copy-start
  1.4 0.1 reshape.43
  1.5 0.6 scatter.4.spots
  2.1 1.8 convert_element_type.3.block
  3.9 60.5 %gather.1 = (bf16[16,2,256,256]{3,2,1,0:T(8,128)(2,1)}, bf16[4,2,256,256]{3,2,1,0:T(8,128)(2,1)}, s32[16,8,128]{2,1,0:T(8,128)}, f32[256,256]{1,0:T(8,128)}, f32...) custom-call(bf16[2,256,256]{2,1,0:T(8,128)(2,1)} %convert_element_type.3.block, s32[8,128]{1,0:T(8,128)} %scatter.4.spots, ...), custom_call_target="tpu_custom_call" | custom-call | tf_op jit(solution)/shard_map/gather/pallas_call | solution.py:414
  64.4 0.9 slice_reduce_fusion
  65.3 0.7 reshape_squeeze.3.pos
  65.9 0.0 copy-done
  65.9 55.1 %project.1 = (s16[16,272,256]{2,1,0:T(8,128)(2,1)}, f32[17,256,256]{2,1,0:T(8,128)}) custom-call(s32[4,2]{1,0:T(4,128)} %copy-done, bf16[16,2,256,256]{3,2,1,0:T(8,128)(2,1)} %get-tuple-element.25.near.far_block, bf16[16,2,256,256]{3,2,1,0:T(8,128)(2,1)} %get-tuple-element.25.near.far_block, bf16[4,2,256,256]{3,2,1,0:T(8,128)(2,1)} %get-tuple-element.26.below, ...), custom_call_target="tpu_custom_call" | custom-call | tf_op jit(solution)/shard_map/project/pallas_call | solution.py:187
  121.1 103.4 %finish.1 = (f32[2,256,256]{2,1,0:T(8,128)}, f32[16,256,256]{2,1,0:T(8,128)}) custom-call(s32[64,2]{1,0:T(8,128)} %reshape_squeeze.3.pos, s16[16,272,256]{2,1,0:T(8,128)(2,1)} %get-tuple-element.29.slots, f32[17,256,256]{2,1,0:T(8,128)} %get-tuple-element.30.sums, f32[16,256,256]{2,1,0:T(8,128)} %bitcast.3, f32[2,256,256]{2,1,0:T(8,128)} %field.1, ...), custom_call_target="tpu_custom_call" | custom-call | tf_op jit(solution)/shard_map/finish/pallas_call | solution.py:675
  224.5 1.9 copy.13
  226.4 4.6 %copy.14 = f32[8,2,256,256]{3,2,1,0:T(8,128)} copy(f32[8,2,256,256]{3,2,1,0:T(8,128)} %bitcast.4) | data formatting | bytes 8388608
Async XLA Ops:
  1.4 64.6 %copy-start = (s32[4,2]{1,0:T(4,128)}, s32[4,2]{1,0:T(4,128)S(1)}, u32[]{:S(2)}) copy-start(s32[4,2]{1,0:T(4,128)S(1)} %copy.9.pos) | copy-start | bytes 100

commit v4 on v0

v4 whole, which is shorter than its diff:
```python
import functools
import math

import jax
import jax.numpy as jnp
import ml_dtypes
import numpy as np
from jax import lax
from jax.experimental import pallas as pl
from jax.experimental.pallas import tpu as pltpu
from jax.sharding import PartitionSpec as P

F32 = jnp.float32
BF16 = jnp.bfloat16
N = 256
H = N // 2
I16 = jnp.int16
TAIL = 16
GROUPS = 4
UNROLL = 4
STRIP = 32
FULL = 32767.0
MESH = pl.DeviceIdType.MESH


def folded_tables():
    counter = np.arange(N, dtype=np.int32)
    phase = counter[:, None] * counter[None, :] % N
    angle = phase.astype(np.float32) * np.float32(2.0 * math.pi / N)
    factor = np.float32(1.0 / math.sqrt(N))
    cosine = (np.cos(angle) * factor).astype(ml_dtypes.bfloat16)
    sine = (np.sin(angle) * factor).astype(ml_dtypes.bfloat16)
    order = np.where(counter <= H, counter, 3 * H - counter)
    right = np.concatenate([cosine[:, : H + 1], sine[:, 1:H]], axis=1)[order]
    return np.stack([right, np.ascontiguousarray(right.T)])


def dot(left, right):
    return jnp.dot(left, right, preferred_element_type=F32)


def iota(axis):
    return lax.broadcasted_iota(jnp.int32, (N, N), axis)


def folded(index):
    return jnp.where(index <= H, index, 3 * H - index)


def one_hot(condition):
    return jnp.where(condition, 1.0, 0.0).astype(BF16)


def pieces(value, count):
    parts = []
    for _ in range(count):
        part = value.astype(BF16)
        parts.append(part)
        value = value - part.astype(F32)
    return parts


def permute(value, left, right, count):
    rows = sum(dot(left, part) for part in pieces(value, count))
    return sum(dot(part, right) for part in pieces(rows, count))


def encode(value):
    size = jnp.abs(value)
    peak = jnp.maximum(jnp.max(size, axis=0, keepdims=True), 1e-30)
    exponent = jnp.ceil(jnp.log(peak) * (1.0 / math.log(2.0)) + 1e-5)
    scale = jnp.exp(exponent * -math.log(2.0))
    code = jnp.minimum(jnp.sqrt(size * scale) * FULL + 0.5, FULL).astype(jnp.int32)
    code = jnp.where(value < 0.0, -code, code).astype(I16)
    tail = jnp.broadcast_to(exponent.astype(jnp.int32), (TAIL, value.shape[1])).astype(I16)
    return code, tail


def decode_scale(tail):
    exponent = tail.astype(jnp.int32).astype(F32)[:1]
    return jnp.exp(exponent * math.log(2.0)) * (1.0 / (FULL * FULL))


def decode(code, scale):
    code = code.astype(jnp.int32).astype(F32)
    return code * jnp.abs(code) * scale


def fold(a_lo, a_hi, b_lo, b_hi, sign, first):
    if first is None:
        return a_lo - sign * b_hi, b_lo + sign * a_hi, a_lo + sign * b_hi, b_lo - sign * a_hi
    a_in = jnp.where(first, 0.0, a_hi)
    b_in = jnp.where(first, 0.0, b_hi)
    return (
        a_lo - sign * b_in,
        b_lo + sign * a_in,
        jnp.where(first, a_hi, a_lo + sign * b_hi),
        jnp.where(first, b_hi, b_lo - sign * a_hi),
    )


def right_stage(re, im, table, half, sign):
    both = dot(jnp.concatenate([re, im], axis=0), table)
    a, b = both[:N], both[N:]
    first = lax.broadcasted_iota(jnp.int32, (N, H), 1) == 0
    re_lo, im_lo, re_hi, im_hi = fold(a[:, :H], a[:, H:], b[:, :H], b[:, H:], sign, first)
    half[:, :H] = re_lo.astype(BF16)
    half[:, H:N] = re_hi.astype(BF16)
    half[:, N : N + H] = im_lo.astype(BF16)
    half[:, N + H :] = im_hi.astype(BF16)


def left_strip(flat, at, sign):
    first = lax.broadcasted_iota(jnp.int32, (STRIP, N), 0) == 0 if at == 0 else None
    low, high = slice(at, at + STRIP), slice(H + at, H + at + STRIP)
    re_lo, im_lo, re_hi, im_hi = fold(flat[low, :N], flat[high, :N], flat[low, N:], flat[high, N:], sign, first)
    return (low, re_lo, im_lo), (high, re_hi, im_hi)


def remote(src, dst, send, recv, scan, tile):
    return pltpu.make_async_remote_copy(
        src_ref=src,
        dst_ref=dst,
        send_sem=send,
        recv_sem=recv,
        device_id={"scan": scan, "tile": tile},
        device_id_type=MESH,
    )


def greet():
    scan_count, tile_count = lax.axis_size("scan"), lax.axis_size("tile")
    me, tile = lax.axis_index("scan"), lax.axis_index("tile")
    barrier = pltpu.get_barrier_semaphore()

    @pl.loop(1, scan_count)
    def _(d):
        pl.semaphore_signal(barrier, 1, device_id={"scan": (me + d) % scan_count, "tile": tile}, device_id_type=MESH)

    @pl.loop(1, tile_count)
    def _(d):
        pl.semaphore_signal(barrier, 1, device_id={"scan": me, "tile": (tile + d) % tile_count}, device_id_type=MESH)

    pl.semaphore_wait(barrier, scan_count + tile_count - 2)


def sweep_kernel(
    field,
    spots,
    table,
    probe,
    patterns,
    coded,
    numer,
    cover,
    block,
    band,
    below,
    cut,
    spots_own,
    spots_above,
    spot_words,
    spot_words_above,
    power_total,
    probe_chunk,
    folded_probe,
    level,
    patch,
    far,
    power,
    halves,
    flats,
    sums,
    update,
    queue,
    slots,
    received,
    core_in,
    x_out,
    x_in,
    y_part,
    y_in,
    z_in,
    den_chunk,
    acc,
    spill_in,
    swap_in,
    tail_in,
    send_sem,
    recv_sem,
    spot_send,
    spot_recv,
    cut_send,
    cut_recv,
    move_send,
    move_recv,
    sum_send,
    sum_recv,
    local_sem,
):
    scan_count, tile_count = lax.axis_size("scan"), lax.axis_size("tile")
    me, tile = lax.axis_index("scan"), lax.axis_index("tile")
    x, core = tile // 2, tile % 2
    y, z = me // 4, me % 4
    pair, parity = me // 2, me % 2
    partner = tile + 1 - 2 * core
    next_tile, last_tile = (tile + 1) % tile_count, (tile + tile_count - 1) % tile_count
    per_device = level.shape[0]
    modes = folded_probe.shape[0] // 2
    other_lanes = pl.ds(pl.multiple_of((1 - core) * H, H), H)
    own_lanes = pl.ds(pl.multiple_of(core * H, H), H)

    probe_load = pltpu.make_async_copy(probe, far.at[0], local_sem.at[0])
    probe_load.start()
    pattern_load = pltpu.make_async_copy(patterns, level, local_sem.at[1])
    pattern_load.start()
    block[...] = field[...].astype(BF16)
    greet()

    def spot_copy(d):
        return remote(spots, spots_own.at[me], spot_send.at[d], spot_recv.at[d], (me + d) % scan_count, tile)

    @pl.loop(1, scan_count)
    def _(d):
        spot_copy(d).start()

    def along(plane, stage, d):
        turn_z = (plane == 0) == (stage == 0)
        return 4 * y + (z + d) % 4 if turn_z else 4 * ((y + d) % 4) + z

    sent = []

    def push(src, source, plane, stage, d):
        move = remote(
            src,
            band.at[source, plane],
            send_sem.at[len(sent)],
            recv_sem.at[2 * source + plane],
            along(plane, stage, d),
            tile,
        )
        move.start()
        sent.append(move)

    for stage in range(2):
        for d in (1, 3, 2):
            for plane in range(2):
                push(block.at[plane], me, plane, stage, d)

    def landed(source, plane):
        remote(
            block.at[plane], band.at[source, plane], send_sem.at[0], recv_sem.at[2 * source + plane], along(0, 0, 1), tile
        ).wait_recv()

    spots_own[me] = spots[...]
    band[me] = block[...]
    probe_load.wait()
    total = jnp.zeros((N, N), F32)
    for m in range(modes):
        for plane in range(2):
            value = far[0, m, plane]
            total = total + value * value
    power_total[...] = total

    for d in (3, 1, 2):
        for plane in range(2):
            source = along(plane, 0, d)
            landed(source, plane)
            for turn in (1, 3, 2):
                push(band.at[source, plane], source, plane, 1, turn)

    @pl.loop(1, scan_count)
    def _(d):
        source = (me + scan_count - d) % scan_count
        remote(spots, spots_own.at[source], spot_send.at[d], spot_recv.at[d], source, tile).wait_recv()

    above_copy = remote(spots_own, spots_above, spot_send.at[0], spot_recv.at[0], me, next_tile)
    above_copy.start()
    words_copy = pltpu.make_async_copy(spots_own, spot_words, local_sem.at[2])
    words_copy.start()

    fold_matrix = one_hot(iota(0) == folded(iota(1)))
    chunk_rows = pl.ds(pl.multiple_of(x * 64 + y * 16, 16), 16)

    @pl.loop(0, modes)
    def _(m):
        for plane in range(2):
            folded_probe[2 * m + plane] = permute(far[0, m, plane], fold_matrix, fold_matrix, 3)
            probe_chunk[2 * m + plane] = far[0, m, plane, chunk_rows, own_lanes]

    pattern_load.wait()

    @pl.loop(0, per_device)
    def _(k):
        level[k] = jnp.sqrt(permute(level[k], fold_matrix, fold_matrix, 3))

    cover[...] = jnp.zeros_like(cover)

    def add_cover(words, above):
        @pl.loop(0, scan_count)
        def _(source):
            head, row_shift, col_shift = jnp.int32(-1), jnp.int32(0), jnp.int32(0)
            for k in range(per_device):
                row, col = words[source, 0, 2 * k], words[source, 0, 2 * k + 1]
                owner = col // N
                first = owner == me
                hit = first | ((owner + 1) % scan_count == me)
                head = jnp.where(hit, first.astype(jnp.int32), head)
                row_shift = jnp.where(hit, row % N, row_shift)
                col_shift = jnp.where(hit, col % N, col_shift)
            start = jnp.where(head == 1, col_shift, 0)
            stop = jnp.where(head == 1, N, jnp.where(head == 0, col_shift, 0))
            rows, cols = iota(0), iota(1)
            moved = pltpu.roll(pltpu.roll(power_total[...], row_shift, 0), col_shift, 1)
            keep = (rows < row_shift) if above else (rows >= row_shift)
            cover[...] += jnp.where(keep & (cols >= start) & (cols < stop), moved, 0.0)

    words_copy.wait()
    add_cover(spot_words, False)
    above_copy.wait_recv()
    words_copy = pltpu.make_async_copy(spots_above, spot_words_above, local_sem.at[3])
    words_copy.start()
    words_copy.wait()
    add_cover(spot_words_above, True)

    for d in (3, 1, 2):
        for plane in range(2):
            for turn in (3, 1, 2):
                if plane == 0:
                    source = 4 * ((y + turn) % 4) + (z + d) % 4
                else:
                    source = 4 * ((y + d) % 4) + (z + turn) % 4
                landed(source, plane)
    for turn in (3, 1, 2):
        landed(4 * ((y + turn) % 4) + z, 0)
        landed(4 * y + (z + turn) % 4, 1)

    def composite(col, plane):
        owner, col_shift = col // N, col % N
        after = (owner + 1) % scan_count
        return jnp.where(iota(1) >= col_shift, band[owner, plane].astype(F32), band[after, plane].astype(F32))

    def cut_copy(k):
        return remote(cut.at[k], below.at[k], cut_send.at[k], cut_recv.at[k], me, last_tile)

    @pl.loop(0, per_device)
    def _(k):
        for plane in range(2):
            cut[k, plane] = composite(spot_words_above[me, 0, 2 * k + 1], plane).astype(BF16)
        cut_copy(k).start()

    update[...] = jnp.zeros_like(update)
    sums[...] = jnp.zeros_like(sums)
    acc[...] = jnp.zeros_like(acc)
    queue[per_device] = jnp.zeros(queue.shape[1:], I16)

    @pl.loop(0, per_device)
    def _(k):
        row, col = spot_words[me, 0, 2 * k], spot_words[me, 0, 2 * k + 1]
        row_shift, col_shift = row % N, col % N
        cut_copy(k).wait_recv()
        row_pick = one_hot(iota(1) == (row_shift + folded(iota(0))) % N)
        col_pick = one_hot(iota(0) == (col_shift + folded(iota(1))) % N)
        for plane in range(2):
            top = composite(col, plane)
            window = jnp.where(iota(0) >= row_shift, top, below[k, plane].astype(F32)).astype(BF16)
            patch[k, plane] = dot(dot(row_pick, window).astype(BF16), col_pick)
        sums[0] += patch[k, 0] * patch[k, 0] + patch[k, 1] * patch[k, 1]
        power[k] = jnp.full((N, N), 0.25, F32)

        @pl.loop(0, modes // UNROLL)
        def _(part):
            for u in range(UNROLL):
                m = part * UNROLL + u
                half, flat = halves.at[u], flats.at[u]
                p_re, p_im = folded_probe[2 * m], folded_probe[2 * m + 1]
                o_re, o_im = patch[k, 0], patch[k, 1]
                wave_re = (p_re * o_re - p_im * o_im).astype(BF16)
                wave_im = (p_re * o_im + p_im * o_re).astype(BF16)
                right_stage(wave_re, wave_im, table[0], half, -1.0)
                flat[...] = dot(table[1], half[...])
                for at in range(0, H, STRIP):
                    for rows, f_re, f_im in left_strip(flat, at, -1.0):
                        far[k, m, 0, rows] = f_re
                        far[k, m, 1, rows] = f_im
                        power[k, rows] += f_re * f_re + f_im * f_im

        power[k] = level[k] / jnp.sqrt(power[k])

    sums[0] = permute(sums[0], fold_matrix, fold_matrix, 2)

    PER_GROUP = 20

    def span(g):
        return (0, 2 * modes // GROUPS + 1) if g == 0 else (1 + g * (2 * modes // GROUPS), 2 * modes // GROUPS)

    def sum_copy(src, dst, g, number, scan=None, tile_to=None):
        return remote(
            src,
            dst,
            sum_send.at[g * PER_GROUP + number],
            sum_recv.at[g * PER_GROUP + number],
            me if scan is None else scan,
            tile if tile_to is None else tile_to,
        )

    def core_copy(g):
        start, count = span(g)
        planes = pl.ds(start, count)
        return sum_copy(sums.at[planes, :, other_lanes], core_in.at[planes], g, 0, tile_to=partner)

    def x_copy(g, d):
        used = pl.ds(0, span(g)[1] * 64 + TAIL)
        return sum_copy(
            x_out.at[g, d - 1, used], x_in.at[g, d - 1, used], g, d, tile_to=2 * ((x + d) % 4) + core
        )

    def y_copy(g, d):
        start, count = span(g)
        planes = pl.ds(start, count)
        rows = pl.ds(pl.multiple_of((y + d) % 4 * 16, 16), 16)
        return sum_copy(
            y_part.at[planes, rows], y_in.at[d - 1, planes], g, 3 + d, scan=4 * ((y + d) % 4) + z
        )

    def z_copy(g, d, source):
        planes = pl.ds(*span(g))
        return sum_copy(z_in.at[source, planes], z_in.at[source, planes], g, 6 + d, scan=4 * y + (z + d) % 4)

    def yg_copy(g, d, source):
        at = core * 16 + x * 4 + source
        return sum_copy(coded.at[at, g], coded.at[at, g], g, 9 + d, scan=4 * ((y + d) % 4) + z)

    def xg_copy(g, d, source):
        at = pl.ds(core * 16 + source * 4, 4)
        return sum_copy(coded.at[at, g], coded.at[at, g], g, 12 + d, tile_to=2 * ((x + d) % 4) + core)

    def cg_copy(g, d, side):
        at = pl.ds(side * 16 + (x + 4 - d) % 4 * 4, 4)
        return sum_copy(coded.at[at, g], coded.at[at, g], g, 16 + d, tile_to=partner)

    def stage_core(g):
        core_copy(g).start()

    def stage_x(g):
        start, count = span(g)
        planes = pl.ds(start, count)
        core_copy(g).wait_recv()
        for d in range(1, 4):
            rows = pl.ds(pl.multiple_of((x + d) % 4 * 64, 64), 64)
            chunk = sums[planes, rows, own_lanes] + core_in[planes, rows]
            code, tail = encode(chunk.reshape(count * 64, H))
            x_out[g, d - 1, : count * 64] = code
            x_out[g, d - 1, count * 64 : count * 64 + TAIL] = tail
            x_copy(g, d).start()
        rows = pl.ds(pl.multiple_of(x * 64, 64), 64)
        y_part[planes] = sums[planes, rows, own_lanes] + core_in[planes, rows]

    def stage_y(g):
        start, count = span(g)
        planes = pl.ds(start, count)
        for d in range(1, 4):
            x_copy(g, d).wait_recv()
            scale = decode_scale(x_in[g, d - 1, count * 64 : count * 64 + TAIL])
            y_part[planes] += decode(x_in[g, d - 1, : count * 64], scale).reshape(count, 64, H)
        for d in range(1, 4):
            y_copy(g, d).start()

    def stage_z(g):
        start, count = span(g)
        planes = pl.ds(start, count)
        chunk = y_part[planes, pl.ds(pl.multiple_of(y * 16, 16), 16)]
        for d in range(1, 4):
            y_copy(g, d).wait_recv()
            chunk = chunk + y_in[d - 1, planes]
        z_in[z, planes] = chunk
        for d in range(1, 4):
            z_copy(g, d, z).start()

    def stage_back(g):
        start, count = span(g)
        planes = pl.ds(start, count)
        for d in range(1, 4):
            z_copy(g, d, (z + 4 - d) % 4).wait_recv()
        whole = z_in[0, planes] + z_in[1, planes] + z_in[2, planes] + z_in[3, planes]
        if g == 0:
            den_chunk[...] = 1.0 / (1.0 + whole[0])
            whole = whole[1:]
        width = 2 * modes // GROUPS
        fresh = (probe_chunk[pl.ds(g * width, width)] + whole) * den_chunk[...][None]
        code, tail = encode(fresh.reshape(width * 16, H))
        at = core * 16 + x * 4 + y
        coded[at, g, : width * 16] = code
        coded[at, g, width * 16 :] = tail
        for d in range(1, 4):
            yg_copy(g, d, y).start()

    def stage_x_back(g):
        for d in range(1, 4):
            yg_copy(g, d, (y + 4 - d) % 4).wait_recv()
        for d in range(1, 4):
            xg_copy(g, d, x).start()
        cg_copy(g, 0, core).start()

    def stage_core_back(g):
        for d in range(1, 4):
            xg_copy(g, d, (x + 4 - d) % 4).wait_recv()
            cg_copy(g, d, core).start()

    def stage_end(g):
        for d in range(4):
            cg_copy(g, d, 1 - core).wait_recv()

    stages = (stage_core, stage_x, stage_y, stage_z, stage_back, stage_x_back, stage_core_back, stage_end)

    def tick(n):
        for number in range(len(stages) - 1, -1, -1):
            if 0 <= n - number < GROUPS:
                stages[number](n - number)

    width = modes // GROUPS

    @pl.loop(0, GROUPS)
    def _(n):
        @pl.loop(0, width)
        def _(part):
            m = n * width + part
            for k in range(per_device):
                half, flat = halves.at[k % UNROLL], flats.at[k % UNROLL]
                scaling = power[k]
                fixed_re = (far[k, m, 0] * scaling).astype(BF16)
                fixed_im = (far[k, m, 1] * scaling).astype(BF16)
                right_stage(fixed_re, fixed_im, table[0], half, 1.0)
                flat[...] = dot(table[1], half[...])
                for at in range(0, H, STRIP):
                    for rows, e_re, e_im in left_strip(flat, at, 1.0):
                        p_re, p_im = folded_probe[2 * m, rows], folded_probe[2 * m + 1, rows]
                        o_re, o_im = patch[k, 0, rows], patch[k, 1, rows]
                        update[k, 0, rows] += p_re * e_re + p_im * e_im
                        update[k, 1, rows] += p_re * e_im - p_im * e_re
                        sums[1 + 2 * m, rows] += o_re * e_re + o_im * e_im
                        sums[2 + 2 * m, rows] += o_re * e_im - o_im * e_re
            for plane in range(2):
                at = 1 + 2 * m + plane
                sums[at] = permute(sums[at], fold_matrix, fold_matrix, 2)

        for step in range(GROUPS):
            @pl.when(n == step)
            def _():
                tick(step)

    @pl.loop(0, per_device)
    def _(k):
        row_shift, col_shift = spot_words[me, 0, 2 * k] % N, spot_words[me, 0, 2 * k + 1] % N
        row_back = one_hot(iota(0) == (row_shift + folded(iota(1))) % N)
        col_back = one_hot(iota(1) == (col_shift + folded(iota(0))) % N)
        for plane in range(2):
            code, tail = encode(permute(update[k, plane], row_back, col_back, 2))
            queue[k, plane, :N] = code
            queue[k, plane, N:] = tail

    @pl.loop(0, scan_count // 2)
    def _(q):
        pick = jnp.int32(per_device)
        for k in range(per_device):
            pick = jnp.where(spot_words[me, 0, 2 * k + 1] // (2 * N) == q, k, pick)
        for plane in range(2):
            slots[2 * q + plane] = queue[pick, plane]

    def update_copy(dy, dz):
        to = 4 * ((y + dy) % 4) + (z + dz) % 4
        j = 4 * dy + dz
        return remote(slots.at[to], received.at[j], move_send.at[j], move_recv.at[j], to, tile)

    hops = (0, 1, 2, 1)
    order = sorted(((dy, dz) for dy in range(4) for dz in range(4) if dy or dz), key=lambda d: -hops[d[0]] - hops[d[1]])
    for dy, dz in order:
        update_copy(dy, dz).start()

    def collect(source, ref):
        owner, row_shift, col_shift = jnp.int32(-4), jnp.int32(0), jnp.int32(0)
        for k in range(per_device):
            spot_row, spot_col = spot_words[source, 0, 2 * k], spot_words[source, 0, 2 * k + 1]
            hit = spot_col // (2 * N) == pair
            owner = jnp.where(hit, spot_col // N, owner)
            row_shift = jnp.where(hit, spot_row % N, row_shift)
            col_shift = jnp.where(hit, spot_col % N, col_shift)
        side = owner - 2 * pair
        cols = lax.broadcasted_iota(jnp.int32, (STRIP, N), 1)
        right = cols >= col_shift
        head = jnp.broadcast_to(side, (STRIP, N)) == 0
        tail = jnp.broadcast_to(side, (STRIP, N)) == 1
        picks = (head & right, (head & ~right) | (tail & right), tail & ~right)
        scale = decode_scale(ref[N:])

        for part in range(0, N, STRIP):
            rows = lax.broadcasted_iota(jnp.int32, (STRIP, N), 0) + part
            value = decode(ref[part : part + STRIP], scale)
            low = rows < row_shift
            for at in range(3):
                taken = jnp.where(picks[at], value, 0.0)
                acc[0, at, part : part + STRIP] += jnp.where(low, 0.0, taken)
                acc[1, at, part : part + STRIP] += jnp.where(low, taken, 0.0)

    def collect_some(picked):
        for dy, dz in picked:
            update_copy(dy, dz).wait_recv()
            collect(4 * ((y + 4 - dy) % 4) + (z + 4 - dz) % 4, received.at[4 * dy + dz])

    collect(me, slots.at[me])
    tick(GROUPS)
    collect_some(order[:5])
    tick(GROUPS + 1)
    collect_some(order[5:10])
    tick(GROUPS + 2)
    collect_some(order[10:])

    spill_copy = remote(acc.at[1], spill_in, move_send.at[16], move_recv.at[16], me, next_tile)
    spill_copy.start()
    tick(GROUPS + 3)
    spill_copy.wait_recv()
    acc[0] += spill_in[...]
    swap_copy = remote(
        acc.at[0, 1 - parity], swap_in, move_send.at[17], move_recv.at[17], me + 1 - 2 * parity, tile
    )
    swap_copy.start()

    def tail_copy(plane):
        to = (me + 2 - parity) % scan_count
        return remote(acc.at[0, 2], tail_in.at[plane], move_send.at[18], move_recv.at[18 + plane], to, tile)

    tail_copy(parity).start()
    tick(GROUPS + 4)
    swap_copy.wait_recv()

    @pl.when(parity == 0)
    def _():
        for plane in range(2):
            tail_copy(plane).wait_recv()
        numer[0] = acc[0, 0] + tail_in[0]
        numer[1] = swap_in[...] + tail_in[1]

    @pl.when(parity == 1)
    def _():
        numer[0] = swap_in[...]
        numer[1] = acc[0, 1]

    for n in range(GROUPS + 5, GROUPS + len(stages)):
        tick(n)

    for move in sent:
        move.wait_send()
    above_copy.wait_send()

    @pl.loop(1, scan_count)
    def _(d):
        spot_copy(d).wait_send()

    @pl.loop(0, per_device)
    def _(k):
        cut_copy(k).wait_send()

    for dy, dz in order:
        update_copy(dy, dz).wait_send()
    spill_copy.wait_send()
    swap_copy.wait_send()
    tail_copy(parity).wait_send()
    for g in range(GROUPS):
        core_copy(g).wait_send()
        cg_copy(g, 0, core).wait_send()
        for d in range(1, 4):
            x_copy(g, d).wait_send()
            y_copy(g, d).wait_send()
            z_copy(g, d, z).wait_send()
            yg_copy(g, d, y).wait_send()
            xg_copy(g, d, x).wait_send()
            cg_copy(g, d, core).wait_send()


def sweep(field, spots, table, probe, patterns, scan_count):
    per_device, modes = patterns.shape[0], probe.shape[0]
    planes = 2 * modes + 1
    width = 2 * modes // GROUPS
    vmem, anywhere = pl.BlockSpec(memory_space=pltpu.VMEM), pl.BlockSpec(memory_space=pl.ANY)
    words = (scan_count,) + spots.shape
    dma, mem = pltpu.SemaphoreType.DMA, pltpu.VMEM
    slot = (N + TAIL, N)
    return pl.pallas_call(
        sweep_kernel,
        in_specs=[vmem, vmem, vmem, anywhere, anywhere],
        out_specs=[vmem, vmem, vmem],
        out_shape=[
            jax.ShapeDtypeStruct((2 * scan_count, GROUPS, width * 16 + TAIL, H), I16),
            jax.ShapeDtypeStruct((2, N, N), F32),
            jax.ShapeDtypeStruct((N, N), F32),
        ],
        scratch_shapes=[
            mem((2, N, N), BF16),
            mem((scan_count, 2, N, N), BF16),
            mem((per_device, 2, N, N), BF16),
            mem((per_device, 2, N, N), BF16),
            mem(words, jnp.int32),
            mem(words, jnp.int32),
            pltpu.SMEM(words, jnp.int32),
            pltpu.SMEM(words, jnp.int32),
            mem((N, N), F32),
            mem((2 * modes, 16, H), F32),
            mem((2 * modes, N, N), F32),
            mem((per_device, N, N), F32),
            mem((per_device, 2, N, N), F32),
            mem((per_device, modes, 2, N, N), F32),
            mem((per_device, N, N), F32),
            mem((UNROLL, N, 2 * N), BF16),
            mem((UNROLL, N, 2 * N), F32),
            mem((planes, N, N), F32),
            mem((per_device, 2, N, N), F32),
            mem((per_device + 1, 2) + slot, I16),
            mem((scan_count,) + slot, I16),
            mem((scan_count,) + slot, I16),
            mem((planes, N, H), F32),
            mem((GROUPS, 3, (width + 1) * 64 + TAIL, H), I16),
            mem((GROUPS, 3, (width + 1) * 64 + TAIL, H), I16),
            mem((planes, 64, H), F32),
            mem((3, planes, 16, H), F32),
            mem((4, planes, 16, H), F32),
            mem((16, H), F32),
            mem((2, 3, N, N), F32),
            mem((3, N, N), F32),
            mem((N, N), F32),
            mem((2, N, N), F32),
            dma((30,)),
            dma((2 * scan_count,)),
            dma((scan_count,)),
            dma((scan_count,)),
            dma((per_device,)),
            dma((per_device,)),
            dma((20,)),
            dma((20,)),
            dma((20 * GROUPS,)),
            dma((20 * GROUPS,)),
            dma((4,)),
        ],
        compiler_params=pltpu.CompilerParams(
            collective_id=0, has_side_effects=True, vmem_limit_bytes=62 * 2**20
        ),
        name="sweep",
    )(field, spots, table, probe, patterns)


def final_kernel(coded, numer, cover, field, object_out, probe_out):
    share = 1.0 / (1.0 + cover[...])
    for plane in range(2):
        object_out[plane] = (field[plane] + numer[plane]) * share
    width = (coded.shape[4] - TAIL) // 16
    for core in range(2):
        for at in range(4):
            for g in range(GROUPS):
                scale = decode_scale(coded[core, 0, at, g, width * 16 :])
                value = decode(coded[core, 0, at, g, : width * 16], scale).reshape(width, 16, H)
                probe_out[width * g : width * (g + 1), 16 * at : 16 * (at + 1), core * H : (core + 1) * H] = value


def final(coded, numer, cover, field, planes):
    coded = coded.reshape((2, 4, 4) + coded.shape[1:])
    rows = N // 4
    return pl.pallas_call(
        final_kernel,
        grid=(4,),
        in_specs=[
            pl.BlockSpec((2, 1) + coded.shape[2:], lambda i: (0, i, 0, 0, 0, 0)),
            pl.BlockSpec((2, rows, N), lambda i: (0, i, 0)),
            pl.BlockSpec((rows, N), lambda i: (i, 0)),
            pl.BlockSpec((2, rows, N), lambda i: (0, i, 0)),
        ],
        out_specs=[
            pl.BlockSpec((2, rows, N), lambda i: (0, i, 0)),
            pl.BlockSpec((planes, rows, N), lambda i: (0, i, 0)),
        ],
        out_shape=[jax.ShapeDtypeStruct((2, N, N), F32), jax.ShapeDtypeStruct((planes, N, N), F32)],
        compiler_params=pltpu.CompilerParams(vmem_limit_bytes=40 * 2**20),
        name="final",
    )(coded, numer, cover, field)


def body(object_field, probe_modes, patterns, positions):
    scan_count = lax.axis_size("scan")
    table = jnp.asarray(folded_tables())
    spots = jnp.zeros((8, 128), jnp.int32).at[0, : positions.size].set(positions.reshape(-1))
    coded, numer, cover = sweep(object_field, spots, table, probe_modes, patterns, scan_count)
    planes = 2 * probe_modes.shape[0]
    object_now, probe_now = final(coded, numer, cover, object_field, planes)
    return (object_now, probe_now.reshape(probe_modes.shape))


def solution(mesh):
    return jax.shard_map(
        body,
        mesh=mesh,
        in_specs=(
            P(None, "tile", "scan"),
            P(),
            P(("scan", "tile"), None, None),
            P(("scan", "tile"), None),
        ),
        out_specs=(P(None, "tile", "scan"), P()),
        check_vma=False,
    )
```

time: 688 us -> 158 us (0.23); the launches traced: 676 us -> 157 us
  local copies, waits for them, and re-layouts: 182 us -> 5.24 us
  Pallas kernels: 0 us -> 151 us
  blocking collectives: 146 us -> 0 us
  matrix products: 130 us -> 0 us
  other arithmetic: 68.6 us -> 0 us
  waiting for transfers between devices: 61.7 us -> 0 us
  loops' own time: 41.8 us -> 0 us
  between operations: 30 us -> 0.67 us
  starting transfers between devices: 15.8 us -> 0 us
    pallas_call x0 -> x2, Pallas kernels: none -> 151 us  [the longest x1 148 us: sweep(): pl.pallas_call(sweep_kernel, in_specs=[vmem, vmem, vmem, anywhere, anywhe...]
    all_gather x1 -> x0, blocking collectives: 146 us -> none  [body(): group_spots = lax.all_gather(positions, 'scan', axis=0, tiled=True)]
    dot_general x65 -> x0, matrix products: 130 us -> none  [the longest x32 76.1 us: product(): jnp.einsum('jk,mkl->mjl', left_op, right_op, preferred_element_type=jnp.f...]
    dynamic_update_slice x16 -> x0, local copies, waits for them, and re-layouts: 85 us -> none  [place(): lax.dynamic_update_slice_in_dim(accum_total, previous + moved_block, row_...]
    all_gather x1 -> x0, waiting for transfers between devices: 56.5 us -> none  [body(): band_rows = lax.all_gather(extended, 'scan', axis=2, tiled=True)]
    another operation x1 -> x0, loops' own time: 41.8 us -> none  [body(): accum_total = lax.fori_loop(0, scan_count, place, accum_start)]
    dynamic_slice x64 -> x0, local copies, waits for them, and re-layouts: 38 us -> none  [the longest x16 9.75 us: place(): row_start = dest_rows[slot_index]]
    or x16 -> x0, other arithmetic: 29.2 us -> none  [place(): dest_first[slot_index] & (column >= col_shift)]
  transfers between devices with their start and end apart: 5 -> 0, of which waited for: 2 -> 0; matrix products, arithmetic and copies ran while one was open for 31% -> 0% of each run, Pallas kernels for 0% -> 0%
where the time goes in v4:
time: 158 us; the launch traced here: 157 us
  Pallas kernels  151 us (96%)
  local copies, waits for them, and re-layouts  5.24 us (3%)
    pallas_call x1, Pallas kernels, sweep(): pl.pallas_call(sweep_kernel, in_specs=[vmem, vmem, vmem, anywhere, anywhe...  148 us
    unnamed x9, local copies, waits for them, and re-layouts  4.55 us

profile of v4, /device:TPU:1, one launch (start us, length us, event | category | flops | bytes accessed | tf_op | source)
XLA Modules:
  0.0 157.3 jit_solution(229473753436253176)
XLA Ops:
  0.6 0.0 copy-start.1
  0.6 0.8 copy.8
  1.5 0.1 reshape.43
  1.5 0.6 scatter.4.spots
  2.2 148.3 %sweep.1 = (s16[32,4,80,128]{3,2,1,0:T(8,128)(2,1)}, f32[2,256,256]{2,1,0:T(8,128)}, f32[256,256]{1,0:T(8,128)}) custom-call(f32[2,256,256]{2,1,0:T(8,128)} %field.3, s32[8,128]{1,0:T(8,128)} %scatter.4.spots, bf16[2,256,256]{2,1,0:T(8,128)(2,1)} %constant.29.clone.table, f32[8,2,256,256]{3,2,1,0:T(8,128)} %probe.1, f32[4,256,256]{2,1,0:T(8,128)} %patterns.1), custom_call_target="tpu_custom_call" | custom-call | tf_op jit(solution)/shard_map/sweep/pallas_call | solution.py:688
  150.5 0.0 copy-done.1
  150.5 0.0 copy-start
  150.5 1.7 %copy-done = s16[32,4,80,128]{3,2,1,0:T(8,128)(2,1)S(1)} copy-done((s16[32,4,80,128]{3,2,1,0:T(8,128)(2,1)S(1)}, s16[32,4,80,128]{3,2,1,0:T(8,128)(2,1)}, u32[]{:S(2)}) %copy-start) | copy-done | bytes 2621464
  152.2 0.0 copy-start.2
  152.2 1.0 copy-done.2
  153.3 0.0 copy-start.3
  153.3 0.9 copy-done.3
  154.2 3.1 %final.1 = (f32[2,256,256]{2,1,0:T(8,128)}, f32[16,256,256]{2,1,0:T(8,128)}) custom-call(s16[2,4,4,4,80,128]{5,4,3,2,1,0:T(8,128)(2,1)S(1)} %bitcast.2, f32[2,256,256]{2,1,0:T(8,128)S(1)} %copy-done.2, f32[256,256]{1,0:T(8,128)S(1)} %copy-done.3, f32[2,256,256]{2,1,0:T(8,128)S(1)} %copy-done.1), custom_call_target="tpu_custom_call" | custom-call | tf_op jit(solution)/shard_map/final/pallas_call | solution.py:766
Async XLA Ops:
  0.6 149.9 %copy-start.1 = (f32[2,256,256]{2,1,0:T(8,128)S(1)}, f32[2,256,256]{2,1,0:T(8,128)}, u32[]{:S(2)}) copy-start(f32[2,256,256]{2,1,0:T(8,128)} %field.3) | copy-start | bytes 1572868
  150.5 1.7 %copy-start = (s16[32,4,80,128]{3,2,1,0:T(8,128)(2,1)S(1)}, s16[32,4,80,128]{3,2,1,0:T(8,128)(2,1)}, u32[]{:S(2)}) copy-start(s16[32,4,80,128]{3,2,1,0:T(8,128)(2,1)} %get-tuple-element.19) | copy-start | bytes 7864324
  152.2 1.0 copy-start.2
  153.3 0.9 copy-start.3

commit v5 on v4

--- a/solution.py
+++ b/solution.py
@@ -183,9 +183,8 @@
     z_in,
     den_chunk,
     acc,
-    spill_in,
-    swap_in,
-    tail_in,
+    merge_out,
+    merge_in,
     send_sem,
     recv_sem,
     spot_send,
@@ -574,8 +573,11 @@
 
     hops = (0, 1, 2, 1)
     order = sorted(((dy, dz) for dy in range(4) for dz in range(4) if dy or dz), key=lambda d: -hops[d[0]] - hops[d[1]])
-    for dy, dz in order:
-        update_copy(dy, dz).start()
+    def launch(picked):
+        for dy, dz in picked:
+            update_copy(dy, dz).start()
+
+    launch(order[:6])
 
     def collect(source, ref):
         owner, row_shift, col_shift = jnp.int32(-4), jnp.int32(0), jnp.int32(0)
@@ -609,43 +611,64 @@
 
     collect(me, slots.at[me])
     tick(GROUPS)
-    collect_some(order[:5])
+    launch(order[6:9])
+    collect_some(order[:3])
     tick(GROUPS + 1)
-    collect_some(order[5:10])
+    launch(order[9:12])
+    collect_some(order[3:6])
     tick(GROUPS + 2)
-    collect_some(order[10:])
-
-    spill_copy = remote(acc.at[1], spill_in, move_send.at[16], move_recv.at[16], me, next_tile)
-    spill_copy.start()
+    launch(order[12:])
+    collect_some(order[6:9])
     tick(GROUPS + 3)
-    spill_copy.wait_recv()
-    acc[0] += spill_in[...]
-    swap_copy = remote(
-        acc.at[0, 1 - parity], swap_in, move_send.at[17], move_recv.at[17], me + 1 - 2 * parity, tile
-    )
-    swap_copy.start()
-
-    def tail_copy(plane):
-        to = (me + 2 - parity) % scan_count
-        return remote(acc.at[0, 2], tail_in.at[plane], move_send.at[18], move_recv.at[18 + plane], to, tile)
-
-    tail_copy(parity).start()
+    collect_some(order[9:12])
     tick(GROUPS + 4)
-    swap_copy.wait_recv()
+    collect_some(order[12:])
+    tick(GROUPS + 5)
+
+    def merge_copy(number, band_at, kind, plane, to):
+        return remote(
+            merge_out.at[number],
+            merge_in.at[band_at, kind, plane],
+            move_send.at[16 + number],
+            move_recv.at[16 + 4 * band_at + 2 * kind + plane],
+            to,
+            (tile + band_at) % tile_count,
+        )
+
+    beside = me + 1 - 2 * parity
+    after_pair = (2 * pair + 2) % scan_count
+    merges = []
+    for number, (band_at, at, kind, to) in enumerate(
+        (
+            (1, 2, 1, after_pair),
+            (1, 1 - parity, 0, beside),
+            (1, parity, 0, me),
+            (0, 2, 1, after_pair),
+            (0, 1 - parity, 0, beside),
+        )
+    ):
+        code, tail = encode(acc[band_at, at])
+        merge_out[number, :N] = code
+        merge_out[number, N:] = tail
+        merges.append(merge_copy(number, band_at, kind, parity, to))
+        merges[-1].start()
+
+    def merged(band_at, kind, plane):
+        merge_copy(0, band_at, kind, plane, beside).wait_recv()
+        ref = merge_in.at[band_at, kind, plane]
+        return decode(ref[:N], decode_scale(ref[N:]))
+
+    numer[1 - parity] = merged(0, 0, 1 - parity)
+    numer[1 - parity] += merged(1, 0, 1 - parity)
+    numer[parity] = acc[0, parity] + merged(1, 0, parity)
 
     @pl.when(parity == 0)
     def _():
-        for plane in range(2):
-            tail_copy(plane).wait_recv()
-        numer[0] = acc[0, 0] + tail_in[0]
-        numer[1] = swap_in[...] + tail_in[1]
-
-    @pl.when(parity == 1)
-    def _():
-        numer[0] = swap_in[...]
-        numer[1] = acc[0, 1]
-
-    for n in range(GROUPS + 5, GROUPS + len(stages)):
+        for band_at in range(2):
+            for plane in range(2):
+                numer[plane] += merged(band_at, 1, plane)
+
+    for n in range(GROUPS + 6, GROUPS + len(stages)):
         tick(n)
 
     for move in sent:
@@ -662,9 +685,8 @@
 
     for dy, dz in order:
         update_copy(dy, dz).wait_send()
-    spill_copy.wait_send()
-    swap_copy.wait_send()
-    tail_copy(parity).wait_send()
+    for move in merges:
+        move.wait_send()
     for g in range(GROUPS):
         core_copy(g).wait_send()
         cg_copy(g, 0, core).wait_send()
@@ -725,17 +747,16 @@
             mem((4, planes, 16, H), F32),
             mem((16, H), F32),
             mem((2, 3, N, N), F32),
-            mem((3, N, N), F32),
-            mem((N, N), F32),
-            mem((2, N, N), F32),
+            mem((5,) + slot, I16),
+            mem((2, 2, 2) + slot, I16),
             dma((30,)),
             dma((2 * scan_count,)),
             dma((scan_count,)),
             dma((scan_count,)),
             dma((per_device,)),
             dma((per_device,)),
-            dma((20,)),
-            dma((20,)),
+            dma((24,)),
+            dma((24,)),
             dma((20 * GROUPS,)),
             dma((20 * GROUPS,)),
             dma((4,)),
@@ -777,7 +798,7 @@
             pl.BlockSpec((planes, rows, N), lambda i: (0, i, 0)),
         ],
         out_shape=[jax.ShapeDtypeStruct((2, N, N), F32), jax.ShapeDtypeStruct((planes, N, N), F32)],
-        compiler_params=pltpu.CompilerParams(vmem_limit_bytes=40 * 2**20),
+        compiler_params=pltpu.CompilerParams(vmem_limit_bytes=62 * 2**20),
         name="final",
     )(coded, numer, cover, field)
 

time: 158 us -> 153 us (0.968)
  local copies, waits for them, and re-layouts: 5.24 us -> 1.45 us
    pallas_call x1, Pallas kernels: 148 us -> 144 us  [sweep(): pl.pallas_call(sweep_kernel, in_specs=[vmem, vmem, vmem, anywhere, anywhe...]
    unnamed x9 -> x1, local copies, waits for them, and re-layouts: 4.55 us -> 0.77 us
    pallas_call x1, Pallas kernels: 3.07 us -> 5.03 us  [final(): pl.pallas_call(final_kernel, grid=(4,), in_specs=[pl.BlockSpec((2, 1) + c...]
where the time goes in v5:
time: 153 us; the launch traced here: 152 us
  Pallas kernels  150 us (98%)
    pallas_call x1, Pallas kernels, sweep(): pl.pallas_call(sweep_kernel, in_specs=[vmem, vmem, vmem, anywhere, anywhe...  144 us
    pallas_call x1, Pallas kernels, final(): pl.pallas_call(final_kernel, grid=(4,), in_specs=[pl.BlockSpec((2, 1) + c...  5.03 us

profile of v5, /device:TPU:1, one launch (start us, length us, event | category | flops | bytes accessed | tf_op | source)
XLA Modules:
  0.0 151.6 jit_solution(16706273958114898726)
XLA Ops:
  0.6 0.8 copy.8
  1.4 0.1 reshape.43
  1.5 0.6 scatter.4.spots
  2.1 144.5 %sweep.1 = (s16[32,4,80,128]{3,2,1,0:T(8,128)(2,1)}, f32[2,256,256]{2,1,0:T(8,128)}, f32[256,256]{1,0:T(8,128)}) custom-call(f32[2,256,256]{2,1,0:T(8,128)} %field.3, s32[8,128]{1,0:T(8,128)} %scatter.4.spots, bf16[2,256,256]{2,1,0:T(8,128)(2,1)} %constant.29.clone.table, f32[8,2,256,256]{3,2,1,0:T(8,128)} %probe.1, f32[4,256,256]{2,1,0:T(8,128)} %patterns.1), custom_call_target="tpu_custom_call" | custom-call | tf_op jit(solution)/shard_map/sweep/pallas_call | solution.py:710
  146.6 5.0 %final.1 = (f32[2,256,256]{2,1,0:T(8,128)}, f32[16,256,256]{2,1,0:T(8,128)}) custom-call(s16[2,4,4,4,80,128]{5,4,3,2,1,0:T(8,128)(2,1)} %bitcast.2, f32[2,256,256]{2,1,0:T(8,128)} %get-tuple-element.20.numer, f32[256,256]{1,0:T(8,128)} %get-tuple-element.21.cover, f32[2,256,256]{2,1,0:T(8,128)} %field.3), custom_call_target="tpu_custom_call" | custom-call | tf_op jit(solution)/shard_map/final/pallas_call | solution.py:787

commit v6 on v5

--- a/solution.py
+++ b/solution.py
@@ -84,6 +84,13 @@
 def decode(code, scale):
     code = code.astype(jnp.int32).astype(F32)
     return code * jnp.abs(code) * scale
+
+
+def unfold(value, flip):
+    high = sum(dot(flip, part) for part in pieces(value[H:], 2))
+    rows = jnp.concatenate([value[:H], high], axis=0)
+    right = sum(dot(part, flip) for part in pieces(rows[:, H:], 2))
+    return jnp.concatenate([rows[:, :H], right], axis=1)
 
 
 def fold(a_lo, a_hi, b_lo, b_hi, sign, first):
@@ -386,7 +393,10 @@
 
         power[k] = level[k] / jnp.sqrt(power[k])
 
-    sums[0] = permute(sums[0], fold_matrix, fold_matrix, 2)
+    half_rows = lax.broadcasted_iota(jnp.int32, (H, H), 0)
+    half_cols = lax.broadcasted_iota(jnp.int32, (H, H), 1)
+    flip = one_hot(half_rows == (H - half_cols) % H)
+    sums[0] = unfold(sums[0], flip)
 
     PER_GROUP = 20
 
@@ -541,15 +551,14 @@
                         sums[2 + 2 * m, rows] += o_re * e_im - o_im * e_re
             for plane in range(2):
                 at = 1 + 2 * m + plane
-                sums[at] = permute(sums[at], fold_matrix, fold_matrix, 2)
+                sums[at] = unfold(sums[at], flip)
 
         for step in range(GROUPS):
             @pl.when(n == step)
             def _():
                 tick(step)
 
-    @pl.loop(0, per_device)
-    def _(k):
+    def file_update(k):
         row_shift, col_shift = spot_words[me, 0, 2 * k] % N, spot_words[me, 0, 2 * k + 1] % N
         row_back = one_hot(iota(0) == (row_shift + folded(iota(1))) % N)
         col_back = one_hot(iota(1) == (col_shift + folded(iota(0))) % N)
@@ -558,6 +567,10 @@
             queue[k, plane, :N] = code
             queue[k, plane, N:] = tail
 
+    pl.loop(0, per_device // 2)(file_update)
+    tick(GROUPS)
+    pl.loop(per_device // 2, per_device)(file_update)
+
     @pl.loop(0, scan_count // 2)
     def _(q):
         pick = jnp.int32(per_device)
@@ -577,6 +590,7 @@
         for dy, dz in picked:
             update_copy(dy, dz).start()
 
+    tick(GROUPS + 1)
     launch(order[:6])
 
     def collect(source, ref):
@@ -610,20 +624,19 @@
             collect(4 * ((y + 4 - dy) % 4) + (z + 4 - dz) % 4, received.at[4 * dy + dz])
 
     collect(me, slots.at[me])
-    tick(GROUPS)
+    tick(GROUPS + 2)
     launch(order[6:9])
     collect_some(order[:3])
-    tick(GROUPS + 1)
+    tick(GROUPS + 3)
     launch(order[9:12])
     collect_some(order[3:6])
-    tick(GROUPS + 2)
+    tick(GROUPS + 4)
     launch(order[12:])
     collect_some(order[6:9])
-    tick(GROUPS + 3)
+    tick(GROUPS + 5)
     collect_some(order[9:12])
-    tick(GROUPS + 4)
+    tick(GROUPS + 6)
     collect_some(order[12:])
-    tick(GROUPS + 5)
 
     def merge_copy(number, band_at, kind, plane, to):
         return remote(
@@ -668,8 +681,6 @@
             for plane in range(2):
                 numer[plane] += merged(band_at, 1, plane)
 
-    for n in range(GROUPS + 6, GROUPS + len(stages)):
-        tick(n)
 
     for move in sent:
         move.wait_send()

time: 153 us -> 151 us (0.987)
  Pallas kernels: 150 us -> 147 us
    pallas_call x1, Pallas kernels: 144 us -> 142 us  [sweep(): pl.pallas_call(sweep_kernel, in_specs=[vmem, vmem, vmem, anywhere, anywhe...]
where the time goes in v6:
time: 151 us; the launch traced here: 149 us
  Pallas kernels  147 us (97%)
    pallas_call x1, Pallas kernels, sweep(): pl.pallas_call(sweep_kernel, in_specs=[vmem, vmem, vmem, anywhere, anywhe...  142 us
    pallas_call x1, Pallas kernels, final(): pl.pallas_call(final_kernel, grid=(4,), in_specs=[pl.BlockSpec((2, 1) + c...  5.03 us

profile of v6, /device:TPU:1, one launch (start us, length us, event | category | flops | bytes accessed | tf_op | source)
XLA Modules:
  0.0 149.3 jit_solution(13190381384049791129)
XLA Ops:
  0.6 0.8 copy.8
  1.4 0.1 reshape.43
  1.5 0.6 scatter.4.spots
  2.1 142.2 %sweep.1 = (s16[32,4,80,128]{3,2,1,0:T(8,128)(2,1)}, f32[2,256,256]{2,1,0:T(8,128)}, f32[256,256]{1,0:T(8,128)}) custom-call(f32[2,256,256]{2,1,0:T(8,128)} %field.3, s32[8,128]{1,0:T(8,128)} %scatter.4.spots, bf16[2,256,256]{2,1,0:T(8,128)(2,1)} %constant.29.clone.table, f32[8,2,256,256]{3,2,1,0:T(8,128)} %probe.1, f32[4,256,256]{2,1,0:T(8,128)} %patterns.1), custom_call_target="tpu_custom_call" | custom-call | tf_op jit(solution)/shard_map/sweep/pallas_call | solution.py:721
  144.3 5.0 %final.1 = (f32[2,256,256]{2,1,0:T(8,128)}, f32[16,256,256]{2,1,0:T(8,128)}) custom-call(s16[2,4,4,4,80,128]{5,4,3,2,1,0:T(8,128)(2,1)} %bitcast.2, f32[2,256,256]{2,1,0:T(8,128)} %get-tuple-element.20.numer, f32[256,256]{1,0:T(8,128)} %get-tuple-element.21.cover, f32[2,256,256]{2,1,0:T(8,128)} %field.3), custom_call_target="tpu_custom_call" | custom-call | tf_op jit(solution)/shard_map/final/pallas_call | solution.py:798

commit v7 on v6

--- a/solution.py
+++ b/solution.py
@@ -633,9 +633,7 @@
     tick(GROUPS + 4)
     launch(order[12:])
     collect_some(order[6:9])
-    tick(GROUPS + 5)
     collect_some(order[9:12])
-    tick(GROUPS + 6)
     collect_some(order[12:])
 
     def merge_copy(number, band_at, kind, plane, to):
@@ -665,6 +663,7 @@
         merge_out[number, N:] = tail
         merges.append(merge_copy(number, band_at, kind, parity, to))
         merges[-1].start()
+    tick(GROUPS + 5)
 
     def merged(band_at, kind, plane):
         merge_copy(0, band_at, kind, plane, beside).wait_recv()
@@ -681,6 +680,8 @@
             for plane in range(2):
                 numer[plane] += merged(band_at, 1, plane)
 
+
+    tick(GROUPS + 6)
 
     for move in sent:
         move.wait_send()

time: 151 us -> 150 us (level)
    pallas_call x1, Pallas kernels: 142 us -> 141 us  [sweep(): pl.pallas_call(sweep_kernel, in_specs=[vmem, vmem, vmem, anywhere, anywhe...]
where the time goes in v7:
time: 150 us; the launch traced here: 148 us
  Pallas kernels  146 us (97%)
    pallas_call x1, Pallas kernels, sweep(): pl.pallas_call(sweep_kernel, in_specs=[vmem, vmem, vmem, anywhere, anywhe...  141 us
    pallas_call x1, Pallas kernels, final(): pl.pallas_call(final_kernel, grid=(4,), in_specs=[pl.BlockSpec((2, 1) + c...  5.03 us

profile of v7, /device:TPU:1, one launch (start us, length us, event | category | flops | bytes accessed | tf_op | source)
XLA Modules:
  0.0 147.8 jit_solution(169564264597514314)
XLA Ops:
  0.6 0.8 copy.8
  1.4 0.1 reshape.43
  1.5 0.6 scatter.4.spots
  2.1 140.7 %sweep.1 = (s16[32,4,80,128]{3,2,1,0:T(8,128)(2,1)}, f32[2,256,256]{2,1,0:T(8,128)}, f32[256,256]{1,0:T(8,128)}) custom-call(f32[2,256,256]{2,1,0:T(8,128)} %field.3, s32[8,128]{1,0:T(8,128)} %scatter.4.spots, bf16[2,256,256]{2,1,0:T(8,128)(2,1)} %constant.29.clone.table, f32[8,2,256,256]{3,2,1,0:T(8,128)} %probe.1, f32[4,256,256]{2,1,0:T(8,128)} %patterns.1), custom_call_target="tpu_custom_call" | custom-call | tf_op jit(solution)/shard_map/sweep/pallas_call | solution.py:722
  142.7 5.0 %final.1 = (f32[2,256,256]{2,1,0:T(8,128)}, f32[16,256,256]{2,1,0:T(8,128)}) custom-call(s16[2,4,4,4,80,128]{5,4,3,2,1,0:T(8,128)(2,1)} %bitcast.2, f32[2,256,256]{2,1,0:T(8,128)} %get-tuple-element.20.numer, f32[256,256]{1,0:T(8,128)} %get-tuple-element.21.cover, f32[2,256,256]{2,1,0:T(8,128)} %field.3), custom_call_target="tpu_custom_call" | custom-call | tf_op jit(solution)/shard_map/final/pallas_call | solution.py:799
